TPU v7x, 512 devices: a whole 4x4x16 slice. The times are simulated.
512 devices in a mesh: space: 64 (over z_lo, y, core), snap: 8 (over z_hi, x).
Axes of the slice: x: 4, y: 4, z: 16 (z_hi: 2, z_lo: 8; z = z_hi * 8 + z_lo), core: 2. Of those that a mesh axis runs over, the one named last changes fastest.
Arguments:
- snapshots: float32 [32768, 2048], P('space', 'snap'), may hold values from -6 to 6
- following: float32 [32768], P('space'), may hold values from -6 to 6
- mass: float32 [32768], P('space'), may hold values from 9.155274e-06 to 9.1552734e-05
Outputs:
- gram: float32 [2048, 2048], P('space', 'snap')
- lagged_gram: float32 [2048, 2048], P('space', 'snap')
All inputs are finite; a program needn't handle non-finite values.
Results may differ from a plain program's by a relative error of at most 0.00005.
Values sent between devices are 32-bit elements; how exact they have to be, the bound alone decides.
No kernel may reach another device: no remote copies, remote signals or barrier semaphores. Data moves between devices by JAX's collectives and lax.ppermute only.
A program may use at most 64 MiB of HBM per device.

v0:
```python
import jax
import jax.numpy as jnp
from jax import lax
from jax.sharding import PartitionSpec as P


def from_behind(value, axis, steps):
    count = lax.axis_size(axis)
    leading, last = (max(0, -steps), min(count, count - steps))
    return lax.ppermute(value, axis, [(source, source + steps) for source in range(leading, last)])


def shards(snapshots, following, mass):
    width = snapshots.shape[1]
    window = lax.all_gather(snapshots, "snap", axis=1, tiled=True)
    weighted = mass[:, None] * window
    index = lax.axis_index("snap")
    last = lax.axis_size("snap") - 1
    incoming = from_behind(snapshots[:, 0], "snap", -1)
    nextcol = jnp.where(index == last, following, incoming)
    dims = (((0,), (0,)), ((), ()))
    rows = window.shape[1] // lax.axis_size("space")
    successors = jnp.concatenate([snapshots[:, 1:], nextcol[:, None]], axis=1)
    both = jnp.concatenate([snapshots, successors], axis=1)
    summed = lax.psum(
        lax.dot_general(
            weighted,
            both,
            dims,
            precision=lax.Precision.HIGHEST,
            preferred_element_type=jnp.float32,
        ),
        "space",
    )
    first = lax.axis_index("space") * rows
    mine = lax.dynamic_slice_in_dim(summed, first, rows, 0)
    return (mine[:, :width], mine[:, width:])


def solution(mesh):
    return jax.shard_map(
        shards,
        mesh=mesh,
        in_specs=(P("space", "snap"), P("space"), P("space")),
        out_specs=(P("space", "snap"), P("space", "snap")),
        check_vma=False,
    )
```

profile of v0, /device:TPU:1, one launch (start us, length us, event | category | flops | bytes accessed | tf_op | source)
XLA Modules:
  0.0 1050.7 jit_solution(1879870633603099300)
XLA Ops:
  7.2 0.0 all-gather.2.cloned.1.call-start
  7.2 0.7 all-gather.2.cloned.1.call-update
  7.9 0.0 all-reduce.2.cloned.1.call-start
  7.9 1.1 slice_reduce_fusion
  9.0 1.3 collective-permute-start
  10.3 1.2 slice.12
  11.6 2.4 collective-permute-done
  14.0 0.1 copy.5
  14.1 185.0 %all-gather.2.cloned.1.call-done = f32[512,2048]{1,0:T(8,128)} async-done(((f32[512,256]{1,0:T(8,128)}), f32[512,2048]{1,0:T(8,128)}) %all-gather.2.cloned.1.call-update) | async-done | bytes 4194320 | tf_op jit(solution)/shard_map/all_gather | solution.py:15
  199.1 10.8 %fusion = f32[2048,512]{1,0:T(8,128)} fusion(f32[512,2048]{1,0:T(8,128)} %all-gather.2.cloned.1.call-done, f32[512]{0:T(512)} %param.5, f32[512,1]{1,0:T(8,128)S(1)} %copy.5, f32[512,255]{1,0:T(8,128)S(1)} %slice.12, f32[512,256]{1,0:T(8,128)} %param.3), kind=kOutput, calls=%fused_computation | convolution fusion | flops 6444023808 | bytes 9439232 | tf_op jit(solution)/shard_map/dot_general | solution.py:26
  210.0 0.0 all-reduce.2.cloned.1.call-update
  210.0 832.4 %all-reduce.2.cloned.1.call-done = f32[2048,512]{1,0:T(8,128)} async-done(((f32[2048,512]{1,0:T(8,128)}), f32[2048,512]{1,0:T(8,128)}) %all-reduce.2.cloned.1.call-update) | async-done | bytes 4194320 | tf_op jit(solution)/shard_map/psum | solution.py:25
  1042.4 1.4 fusion.9
  (1 shorter events, 0.0 us)
Async XLA Ops:
  7.2 192.0 %all-gather.2.cloned.1.call-start = ((), (), s32[]{:S(2)}) async-start(), calls=%async_computation | async-start | bytes 4718592 | tf_op jit(solution)/shard_map/all_gather | solution.py:15
  7.9 1034.5 %all-reduce.2.cloned.1.call-start = ((), (), s32[]{:S(2)}) async-start(), calls=%async_computation.1 | async-start | bytes 8388608 | tf_op jit(solution)/shard_map/psum | solution.py:25
  9.0 4.9 collective-permute-start
Sparse Core Ops, SparseCore 0:
  11.1 188.0 all-gather.1
  210.1 832.2 all-reduce.1
where the time goes:
time: 1050 us
  waiting for transfers between devices  1020 us (97%)
  between operations  14.1 us (1%)
  matrix products  10.8 us (1%)
    psum x1, waiting for transfers between devices, shards(): lax.psum(lax.dot_general(weighted, both, dims, precision=lax.Precision.HI...  832 us
    all_gather x1, waiting for transfers between devices, shards(): window = lax.all_gather(snapshots, 'snap', axis=1, tiled=True)  185 us
  transfers between devices with their start and end apart: 3, of which 3 were waited for; matrix products, arithmetic and copies ran while one was open for 0% of the time, Pallas kernels for 0%

commit v1 on v0

v1 whole, which is shorter than its diff:
```python
import jax
import jax.numpy as jnp
import numpy as np
from jax import lax
from jax.sharding import Mesh, PartitionSpec as P

NAMES = ("zl", "y", "c", "zh", "x")
SIZES = (8, 4, 2, 2, 4)
ZL, Y, C, ZH, X = SIZES
FLAT = ZL * Y * C * ZH * X


def routes(move):
    pairs = []
    for source in range(FLAT):
        zl, y, c, zh, x = (int(v) for v in np.unravel_index(source, SIZES))
        target = move(zh * ZL + zl, y, c, x)
        if target is None:
            continue
        z, y, c, x = target
        z = z % (ZH * ZL)
        place = (z % ZL, y % Y, c % C, z // ZL, x % X)
        pairs.append((source, int(np.ravel_multi_index(place, SIZES))))
    return pairs


def send(value, move):
    return lax.ppermute(value, NAMES, routes(move))


def columns_on(step):
    def move(z, y, c, x):
        block = (z // ZL * X + x - step) % (ZH * X)
        return (block // X * ZL + z % ZL, y, c, block % X)

    return move


def across(z, y, c, x):
    return (z + ZL, y, c, x)


def home(z, y, c, x):
    half = ZL // 2
    if half <= z < ZL:
        return (z + half, y, c, x)
    if ZL <= z < ZL + half:
        return (z - half, y, c, x)
    return None


def product(rows, columns):
    return lax.dot_general(
        rows,
        columns,
        (((0,), (0,)), ((), ())),
        precision=lax.Precision.HIGH,
        preferred_element_type=jnp.float32,
    )


def shards(snapshots, following, mass):
    points, width = snapshots.shape
    r = width // (Y * C)
    x, zh, zl = lax.axis_index("x"), lax.axis_index("zh"), lax.axis_index("zl")
    block = zh * X + x

    partner = send(snapshots, across)
    blocks = [snapshots] + [
        send(snapshots, lambda z, y, c, x, k=k: (z, y, c, x - k)) for k in (1, 3, 2)
    ]
    blocks = [blocks[0], blocks[1], blocks[3], blocks[2]]
    first = snapshots[:, 0]
    after_own = send(first, columns_on(1))
    after_partner = send(first, columns_on(X + 1))
    after_own = jnp.where(block == ZH * X - 1, following, after_own)
    after_partner = jnp.where(block == X - 1, following, after_partner)

    after = jnp.stack([after_own, after_partner], axis=1) * mass[:, None]
    edge = jnp.stack([product(after, b) for b in blocks])
    edge = edge.reshape(X, 2, Y * C, r).transpose(2, 1, 0, 3)
    edge = edge.reshape(Y * C, 1, 2 * X * r)

    def gram(columns):
        return jnp.concatenate(
            [product(b, columns).reshape(1, Y * C, r, width) for b in blocks]
        ).transpose(1, 0, 2, 3).reshape(Y * C, X * r, width)

    def scatter(value):
        moved = lax.all_to_all(value, ("y", "c"), 0, 0, tiled=True)
        return jnp.sum(moved, axis=0)

    own = gram(snapshots * mass[:, None])
    pad = jnp.zeros((Y * C, 7, width), jnp.float32)
    own = scatter(jnp.concatenate([own, edge, pad], axis=1))
    edge = own[X * r].reshape(2, X, r)
    own = own[: X * r].reshape(X, r, width)
    cross = scatter(gram(partner * mass[:, None])).reshape(X, r, width)

    edge = jnp.pad(edge.reshape(2 * X, 1, r), ((0, 0), (0, 7), (0, width - r)))
    both = jnp.concatenate([jnp.concatenate([own, cross]), edge], axis=1)
    slots = [
        lax.dynamic_index_in_dim(
            both, ((s // X + zh) % 2) * X + (s - x + X) % X, 0, keepdims=True
        )
        for s in range(ZL)
    ]
    moved = lax.all_to_all(jnp.concatenate(slots), "zl", 0, 0, tiled=True)
    tile = jnp.sum(moved, axis=0)
    other = send(tile, home)
    tile = jnp.where((zl >= X) == (zh == 0), other, tile)
    tile_gram = tile[:r]
    last = tile[r, :r]
    return tile_gram, jnp.concatenate([tile_gram[:, 1:], last[:, None]], axis=1)


def solution(mesh):
    fine = Mesh(mesh.devices.reshape(SIZES), NAMES)
    rows, columns = ("zl", "y", "c"), ("zh", "x")
    return jax.shard_map(
        shards,
        mesh=fine,
        in_specs=(P(rows, columns), P(rows), P(rows)),
        out_specs=(P(rows, columns), P(rows, columns)),
        check_vma=False,
    )
```

time: 1050 us -> 171 us (0.16)
  the two profiles are of different devices: /device:TPU:1 before, /device:TPU:134 now
where the time goes in v1:
time: 171 us; the launch traced here: 170 us
  waiting for transfers between devices  68 us (40%)
  starting transfers between devices  55.3 us (32%)
  blocking collectives  30.8 us (18%)
  matrix products  7.55 us (4%)
  other arithmetic  4.48 us (3%)
  local copies, waits for them, and re-layouts  2.9 us (2%)
    ppermute x7, starting transfers between devices, send(): return lax.ppermute(value, NAMES, routes(move))  47.3 us
    ppermute x7, waiting for transfers between devices, send(): return lax.ppermute(value, NAMES, routes(move))  40.3 us
    all_to_all x1, blocking collectives, shards(): moved = lax.all_to_all(jnp.concatenate(slots), 'zl', 0, 0, tiled=True)  30.8 us
    all_to_all x2, waiting for transfers between devices, scatter(): moved = lax.all_to_all(value, ('y', 'c'), 0, 0, tiled=True)  27.8 us
    all_to_all x2, starting transfers between devices, scatter(): moved = lax.all_to_all(value, ('y', 'c'), 0, 0, tiled=True)  8.02 us
    dot_general x12, matrix products, product(): lax.dot_general(rows, columns, (((0,), (0,)), ((), ())), precision=lax.Pr...  7.55 us
  transfers between devices with their start and end apart: 9, of which 6 were waited for; matrix products, arithmetic and copies ran while one was open for 5% of the time, Pallas kernels for 0%

profile of v1, /device:TPU:134, one launch (start us, length us, event | category | flops | bytes accessed | tf_op | source)
XLA Modules:
  0.0 170.2 jit_solution(14421190386296458580)
XLA Ops:
  0.7 1.1 slice_reduce_fusion
  1.8 2.7 %collective-permute-start.3 = (f32[512]{0:T(512)S(1)}, f32[512]{0:T(512)S(1)}, u32[]{:S(2)}, u32[]{:S(2)}) collective-permute-start(f32[512]{0:T(512)S(1)} %slice_reduce_fusion), channel_id=1, source_target_pairs={{0,7},{1,0},{2,1},{3,2},{4,3},{5,4},{6,5},{7,6},{8,15},{9,8},{10,9... | collective-permute-start | bytes 6152 | tf_op jit(solution)/shard_map/ppermute | solution.py:28
  4.6 10.9 %collective-permute-start.4 = (f32[512]{0:T(512)S(1)}, f32[512]{0:T(512)S(1)}, u32[]{:S(2)}, u32[]{:S(2)}) collective-permute-start(f32[512]{0:T(512)S(1)} %slice_reduce_fusion), channel_id=1, source_target_pairs={{0,3},{1,4},{2,5},{3,6},{4,7},{5,0},{6,1},{7,2},{8,11},{9,12},{10,... | collective-permute-start | bytes 6152 | tf_op jit(solution)/shard_map/ppermute | solution.py:28
  15.5 2.4 %collective-permute-start = (f32[512,256]{1,0:T(8,128)}, f32[512,256]{1,0:T(8,128)S(1)}, u32[]{:S(2)}, u32[]{:S(2)}) collective-permute-start(f32[512,256]{1,0:T(8,128)} %param.3), channel_id=1, source_target_pairs={{0,3},{1,0},{2,1},{3,2},{4,7},{5,4},{6,5},{7,6},{8,11},{9,8},{10,9... | collective-permute-start | bytes 1572872 | tf_op jit(solution)/shard_map/ppermute | solution.py:28
  17.9 5.9 %collective-permute-start.1 = (f32[512,256]{1,0:T(8,128)}, f32[512,256]{1,0:T(8,128)S(1)}, u32[]{:S(2)}, u32[]{:S(2)}) collective-permute-start(f32[512,256]{1,0:T(8,128)} %param.3), channel_id=1, source_target_pairs={{0,2},{1,3},{2,0},{3,1},{4,6},{5,7},{6,4},{7,5},{8,10},{9,11},{10,... | collective-permute-start | bytes 1572872 | tf_op jit(solution)/shard_map/ppermute | solution.py:28
  23.8 4.5 %collective-permute-start.2 = (f32[512,256]{1,0:T(8,128)}, f32[512,256]{1,0:T(8,128)S(1)}, u32[]{:S(2)}, u32[]{:S(2)}) collective-permute-start(f32[512,256]{1,0:T(8,128)} %param.3), channel_id=1, source_target_pairs={{0,1},{1,2},{2,3},{3,0},{4,5},{5,6},{6,7},{7,4},{8,9},{9,10},{10,1... | collective-permute-start | bytes 1572872 | tf_op jit(solution)/shard_map/ppermute | solution.py:28
  28.3 1.9 %fusion.6 = f32[256,256]{0,1:T(8,128)S(1)} fusion(f32[512,256]{1,0:T(8,128)} %param.3, f32[512]{0:T(512)} %param.5), kind=kOutput, calls=%fused_computation.9 | convolution fusion | flops 201457664 | bytes 788480 | tf_op jit(solution)/shard_map/dot_general | solution.py:53
  30.3 0.1 pad.16.clone
  30.4 10.9 %collective-permute-start.5 = (f32[512,256]{1,0:T(8,128)S(1)}, f32[512,256]{1,0:T(8,128)S(1)}, u32[]{:S(2)}, u32[]{:S(2)}) collective-permute-start(f32[512,256]{1,0:T(8,128)S(1)} %copy-done), channel_id=1, source_target_pairs={{0,4},{1,5},{2,6},{3,7},{4,0},{5,1},{6,2},{7,3},{8,12},{9,13},{10,... | collective-permute-start | bytes 1572872 | tf_op jit(solution)/shard_map/ppermute | solution.py:28
  41.3 0.2 fusion.27
  41.5 0.1 stack.27
  41.6 0.1 copy.26
  41.7 0.2 fusion.26
  41.9 0.1 stack.28
  41.9 0.1 copy.27
  42.0 2.7 %collective-permute-done.1 = f32[512,256]{1,0:T(8,128)S(1)} collective-permute-done((f32[512,256]{1,0:T(8,128)}, f32[512,256]{1,0:T(8,128)S(1)}, u32[]{:S(2)}, u32[]{:S(2)}) %collective-permute-start.1) | collective-permute-done | bytes 524320 | tf_op jit(solution)/shard_map/ppermute | solution.py:28
  44.7 0.2 fusion.25
  44.9 0.1 stack.29
  45.0 0.1 copy.28
  45.0 1.3 collective-permute-done.2
  46.3 0.2 fusion.24
  46.5 0.1 stack.30
  46.6 33.0 %collective-permute-done.5 = f32[512,256]{1,0:T(8,128)S(1)} collective-permute-done((f32[512,256]{1,0:T(8,128)S(1)}, f32[512,256]{1,0:T(8,128)S(1)}, u32[]{:S(2)}, u32[]{:S(2)}) %collective-permute-start.5) | collective-permute-done | bytes 524320 | tf_op jit(solution)/shard_map/ppermute | solution.py:28
  79.7 0.7 fusion.12
  80.4 0.7 fusion.10
  81.1 0.7 fusion.8
  81.8 0.7 fusion.14
  82.5 1.1 pad_maximum_fusion.1
  83.6 4.5 %all-to-all-start.1 = ((f32[8,128,256]{2,1,0:T(8,128)}), f32[8,128,256]{2,1,0:T(8,128)}, u32[]{:S(2)}, u32[]{:S(2)}) async-start(f32[8,128,256]{2,1,0:T(8,128)} %bitcast.31), calls=%async_computation.1 | async-start | bytes 2097152 | tf_op jit(solution)/shard_map/all_to_all | solution.py:90
  88.1 0.7 fusion
  88.8 0.1 reshape.66
  88.9 0.7 fusion.4
  89.6 0.7 fusion.2
  90.3 0.1 pad_maximum_fusion
  90.4 1.1 maximum_maximum_fusion
  91.5 12.6 %all-to-all-done.1 = f32[8,128,256]{2,1,0:T(8,128)} async-done(((f32[8,128,256]{2,1,0:T(8,128)}), f32[8,128,256]{2,1,0:T(8,128)}, u32[]{:S(2)}, u32[]{:S(2)}) %all-to-all-start.1) | async-done | bytes 1048608 | tf_op jit(solution)/shard_map/all_to_all | solution.py:90
  104.1 3.6 %all-to-all-start = ((f32[8,136,256]{2,1,0:T(8,128)}), f32[8,136,256]{2,1,0:T(8,128)S(1)}, u32[]{:S(2)}, u32[]{:S(2)}) async-start(f32[8,136,256]{2,1,0:T(8,128)} %maximum_maximum_fusion), calls=%async_computation | async-start | bytes 2228224 | tf_op jit(solution)/shard_map/all_to_all | solution.py:90
  107.8 1.3 reduce_sum.28
  109.1 15.2 %all-to-all-done = f32[8,136,256]{2,1,0:T(8,128)S(1)} async-done(((f32[8,136,256]{2,1,0:T(8,128)}), f32[8,136,256]{2,1,0:T(8,128)S(1)}, u32[]{:S(2)}, u32[]{:S(2)}) %all-to-all-start) | async-done | bytes 1114144 | tf_op jit(solution)/shard_map/all_to_all | solution.py:90
  124.3 0.1 reduce_sum.27
  124.4 0.1 reshape_reshape_squeeze.3
  124.7 30.8 %all_to_all.15 = f32[8,40,256]{2,1,0:T(8,128)S(1)} all-to-all(f32[8,40,256]{2,1,0:T(8,128)S(1)} %dynamic-slice_dynamic-update-slice_fusion), channel_id=1, replica_groups=mesh['zl'=8,'y'=4,'c'=2,'zh'=2,'x'=4] {'zl'}, dimensions={0} | all-to-all | bytes 655360 | tf_op jit(solution)/shard_map/all_to_all | solution.py:108
  155.5 9.9 %collective-permute-start.6 = (f32[40,256]{1,0:T(8,128)S(1)}, f32[40,256]{1,0:T(8,128)S(1)}, u32[]{:S(2)}, u32[]{:S(2)}) collective-permute-start(f32[40,256]{1,0:T(8,128)S(1)} %reduce_sum.29), channel_id=1, source_target_pairs={{4,256},{5,257},{6,258},{7,259},{12,264},{13,265},{14,266},{15,267... | collective-permute-start | bytes 122888 | tf_op jit(solution)/shard_map/ppermute | solution.py:28
  165.4 3.3 %collective-permute-done.6 = f32[40,256]{1,0:T(8,128)S(1)} collective-permute-done((f32[40,256]{1,0:T(8,128)S(1)}, f32[40,256]{1,0:T(8,128)S(1)}, u32[]{:S(2)}, u32[]{:S(2)}) %collective-permute-start.6) | collective-permute-done | bytes 40992 | tf_op jit(solution)/shard_map/ppermute | solution.py:28
  168.7 0.1 slice.28
  168.8 0.6 slice.27
  169.4 0.1 copy.35
  169.5 0.7 pad_maximum_fusion.2
  (27 shorter events, 0.3 us)
Async XLA Ops:
  0.6 29.7 %copy-start = (f32[512,256]{1,0:T(8,128)S(1)}, f32[512,256]{1,0:T(8,128)}, u32[]{:S(2)}) copy-start(f32[512,256]{1,0:T(8,128)} %param.3) | copy-start | bytes 1572868
  0.6 40.7 %copy-start.1 = (f32[512]{0:T(512)S(1)}, f32[512]{0:T(512)}, u32[]{:S(2)}) copy-start(f32[512]{0:T(512)} %param.5) | copy-start | bytes 6148
  0.7 40.6 %copy-start.2 = (f32[512]{0:T(512)S(1)}, f32[512]{0:T(512)}, u32[]{:S(2)}) copy-start(f32[512]{0:T(512)} %param.4) | copy-start | bytes 6148
  1.8 28.6 %collective-permute-start.3 = (f32[512]{0:T(512)S(1)}, f32[512]{0:T(512)S(1)}, u32[]{:S(2)}, u32[]{:S(2)}) collective-permute-start(f32[512]{0:T(512)S(1)} %slice_reduce_fusion), channel_id=1, source_target_pairs={{0,7},{1,0},{2,1},{3,2},{4,3},{5,4},{6,5},{7,6},{8,15},{9,8},{10,9... | collective-permute-start | bytes 6152 | tf_op jit(solution)/shard_map/ppermute | solution.py:28
  4.6 36.7 %collective-permute-start.4 = (f32[512]{0:T(512)S(1)}, f32[512]{0:T(512)S(1)}, u32[]{:S(2)}, u32[]{:S(2)}) collective-permute-start(f32[512]{0:T(512)S(1)} %slice_reduce_fusion), channel_id=1, source_target_pairs={{0,3},{1,4},{2,5},{3,6},{4,7},{5,0},{6,1},{7,2},{8,11},{9,12},{10,... | collective-permute-start | bytes 6152 | tf_op jit(solution)/shard_map/ppermute | solution.py:28
  15.5 26.2 %collective-permute-start = (f32[512,256]{1,0:T(8,128)}, f32[512,256]{1,0:T(8,128)S(1)}, u32[]{:S(2)}, u32[]{:S(2)}) collective-permute-start(f32[512,256]{1,0:T(8,128)} %param.3), channel_id=1, source_target_pairs={{0,3},{1,0},{2,1},{3,2},{4,7},{5,4},{6,5},{7,6},{8,11},{9,8},{10,9... | collective-permute-start | bytes 1572872 | tf_op jit(solution)/shard_map/ppermute | solution.py:28
  17.9 26.8 %collective-permute-start.1 = (f32[512,256]{1,0:T(8,128)}, f32[512,256]{1,0:T(8,128)S(1)}, u32[]{:S(2)}, u32[]{:S(2)}) collective-permute-start(f32[512,256]{1,0:T(8,128)} %param.3), channel_id=1, source_target_pairs={{0,2},{1,3},{2,0},{3,1},{4,6},{5,7},{6,4},{7,5},{8,10},{9,11},{10,... | collective-permute-start | bytes 1572872 | tf_op jit(solution)/shard_map/ppermute | solution.py:28
  23.8 22.5 %collective-permute-start.2 = (f32[512,256]{1,0:T(8,128)}, f32[512,256]{1,0:T(8,128)S(1)}, u32[]{:S(2)}, u32[]{:S(2)}) collective-permute-start(f32[512,256]{1,0:T(8,128)} %param.3), channel_id=1, source_target_pairs={{0,1},{1,2},{2,3},{3,0},{4,5},{5,6},{6,7},{7,4},{8,9},{9,10},{10,1... | collective-permute-start | bytes 1572872 | tf_op jit(solution)/shard_map/ppermute | solution.py:28
  30.4 49.3 %collective-permute-start.5 = (f32[512,256]{1,0:T(8,128)S(1)}, f32[512,256]{1,0:T(8,128)S(1)}, u32[]{:S(2)}, u32[]{:S(2)}) collective-permute-start(f32[512,256]{1,0:T(8,128)S(1)} %copy-done), channel_id=1, source_target_pairs={{0,4},{1,5},{2,6},{3,7},{4,0},{5,1},{6,2},{7,3},{8,12},{9,13},{10,... | collective-permute-start | bytes 1572872 | tf_op jit(solution)/shard_map/ppermute | solution.py:28
  83.6 20.5 %all-to-all-start.1 = ((f32[8,128,256]{2,1,0:T(8,128)}), f32[8,128,256]{2,1,0:T(8,128)}, u32[]{:S(2)}, u32[]{:S(2)}) async-start(f32[8,128,256]{2,1,0:T(8,128)} %bitcast.31), calls=%async_computation.1 | async-start | bytes 2097152 | tf_op jit(solution)/shard_map/all_to_all | solution.py:90
  104.1 20.2 %all-to-all-start = ((f32[8,136,256]{2,1,0:T(8,128)}), f32[8,136,256]{2,1,0:T(8,128)S(1)}, u32[]{:S(2)}, u32[]{:S(2)}) async-start(f32[8,136,256]{2,1,0:T(8,128)} %maximum_maximum_fusion), calls=%async_computation | async-start | bytes 2228224 | tf_op jit(solution)/shard_map/all_to_all | solution.py:90
  155.5 13.2 %collective-permute-start.6 = (f32[40,256]{1,0:T(8,128)S(1)}, f32[40,256]{1,0:T(8,128)S(1)}, u32[]{:S(2)}, u32[]{:S(2)}) collective-permute-start(f32[40,256]{1,0:T(8,128)S(1)} %reduce_sum.29), channel_id=1, source_target_pairs={{4,256},{5,257},{6,258},{7,259},{12,264},{13,265},{14,266},{15,267... | collective-permute-start | bytes 122888 | tf_op jit(solution)/shard_map/ppermute | solution.py:28

commit v2 on v1

--- a/solution.py
+++ b/solution.py
@@ -70,7 +70,7 @@
         send(snapshots, lambda z, y, c, x, k=k: (z, y, c, x - k)) for k in (1, 3, 2)
     ]
     blocks = [blocks[0], blocks[1], blocks[3], blocks[2]]
-    first = snapshots[:, 0]
+    first, _ = lax.optimization_barrier((snapshots[:, 0], blocks[1]))
     after_own = send(first, columns_on(1))
     after_partner = send(first, columns_on(X + 1))
     after_own = jnp.where(block == ZH * X - 1, following, after_own)
@@ -90,12 +90,13 @@
         moved = lax.all_to_all(value, ("y", "c"), 0, 0, tiled=True)
         return jnp.sum(moved, axis=0)
 
-    own = gram(snapshots * mass[:, None])
+    own = scatter(gram(snapshots * mass[:, None])).reshape(X, r, width)
     pad = jnp.zeros((Y * C, 7, width), jnp.float32)
-    own = scatter(jnp.concatenate([own, edge, pad], axis=1))
-    edge = own[X * r].reshape(2, X, r)
-    own = own[: X * r].reshape(X, r, width)
-    cross = scatter(gram(partner * mass[:, None])).reshape(X, r, width)
+    own, partner = lax.optimization_barrier((own, partner))
+    cross = gram(partner * mass[:, None])
+    cross = scatter(jnp.concatenate([cross, edge, pad], axis=1))
+    edge = cross[X * r].reshape(2, X, r)
+    cross = cross[: X * r].reshape(X, r, width)
 
     edge = jnp.pad(edge.reshape(2 * X, 1, r), ((0, 0), (0, 7), (0, width - r)))
     both = jnp.concatenate([jnp.concatenate([own, cross]), edge], axis=1)

time: 171 us -> 137 us (0.80)
  the two profiles are of different devices: /device:TPU:134 before, /device:TPU:128 now
where the time goes in v2:
time: 137 us; the launch traced here: 136 us
  starting transfers between devices  55.1 us (40%)
  waiting for transfers between devices  38.4 us (28%)
  blocking collectives  27.8 us (20%)
  matrix products  7.56 us (6%)
  other arithmetic  4.53 us (3%)
  local copies, waits for them, and re-layouts  1.88 us (1%)
    ppermute x7, starting transfers between devices, send(): return lax.ppermute(value, NAMES, routes(move))  46.9 us
    all_to_all x1, blocking collectives, shards(): moved = lax.all_to_all(jnp.concatenate(slots), 'zl', 0, 0, tiled=True)  27.8 us
    all_to_all x2, waiting for transfers between devices, scatter(): moved = lax.all_to_all(value, ('y', 'c'), 0, 0, tiled=True)  20.5 us
    ppermute x7, waiting for transfers between devices, send(): return lax.ppermute(value, NAMES, routes(move))  17.9 us
    all_to_all x2, starting transfers between devices, scatter(): moved = lax.all_to_all(value, ('y', 'c'), 0, 0, tiled=True)  8.16 us
    dot_general x12, matrix products, product(): lax.dot_general(rows, columns, (((0,), (0,)), ((), ())), precision=lax.Pr...  7.56 us
  transfers between devices with their start and end apart: 9, of which 6 were waited for; matrix products, arithmetic and copies ran while one was open for 6% of the time, Pallas kernels for 0%

profile of v2, /device:TPU:128, one launch (start us, length us, event | category | flops | bytes accessed | tf_op | source)
XLA Modules:
  0.0 136.4 jit_solution(10161842369837490432)
XLA Ops:
  0.6 4.8 %collective-permute-start = (f32[512,256]{1,0:T(8,128)}, f32[512,256]{1,0:T(8,128)S(1)}, u32[]{:S(2)}, u32[]{:S(2)}) collective-permute-start(f32[512,256]{1,0:T(8,128)} %param.3), channel_id=1, source_target_pairs={{0,3},{1,0},{2,1},{3,2},{4,7},{5,4},{6,5},{7,6},{8,11},{9,8},{10,9... | collective-permute-start | bytes 1572872 | tf_op jit(solution)/shard_map/ppermute | solution.py:28
  5.5 2.7 %collective-permute-start.1 = (f32[512,256]{1,0:T(8,128)}, f32[512,256]{1,0:T(8,128)S(1)}, u32[]{:S(2)}, u32[]{:S(2)}) collective-permute-start(f32[512,256]{1,0:T(8,128)} %param.3), channel_id=1, source_target_pairs={{0,2},{1,3},{2,0},{3,1},{4,6},{5,7},{6,4},{7,5},{8,10},{9,11},{10,... | collective-permute-start | bytes 1572872 | tf_op jit(solution)/shard_map/ppermute | solution.py:28
  8.2 2.8 %collective-permute-start.2 = (f32[512,256]{1,0:T(8,128)}, f32[512,256]{1,0:T(8,128)S(1)}, u32[]{:S(2)}, u32[]{:S(2)}) collective-permute-start(f32[512,256]{1,0:T(8,128)} %param.3), channel_id=1, source_target_pairs={{0,1},{1,2},{2,3},{3,0},{4,5},{5,6},{6,7},{7,4},{8,9},{9,10},{10,1... | collective-permute-start | bytes 1572872 | tf_op jit(solution)/shard_map/ppermute | solution.py:28
  11.0 10.9 %collective-permute-start.3 = (f32[512,256]{1,0:T(8,128)}, f32[512,256]{1,0:T(8,128)S(1)}, u32[]{:S(2)}, u32[]{:S(2)}) collective-permute-start(f32[512,256]{1,0:T(8,128)} %param.3), channel_id=1, source_target_pairs={{0,4},{1,5},{2,6},{3,7},{4,0},{5,1},{6,2},{7,3},{8,12},{9,13},{10,... | collective-permute-start | bytes 1572872 | tf_op jit(solution)/shard_map/ppermute | solution.py:28
  21.9 1.9 %fusion.6 = f32[256,256]{0,1:T(8,128)S(1)} fusion(f32[512,256]{1,0:T(8,128)} %param.3, f32[512]{0:T(512)} %param.5), kind=kOutput, calls=%fused_computation.9 | convolution fusion | flops 201457664 | bytes 788480 | tf_op jit(solution)/shard_map/dot_general | solution.py:53
  23.8 0.1 slice_reduce_fusion
  24.0 0.1 pad.12.clone
  24.1 4.1 %collective-permute-done = f32[512,256]{1,0:T(8,128)S(1)} collective-permute-done((f32[512,256]{1,0:T(8,128)}, f32[512,256]{1,0:T(8,128)S(1)}, u32[]{:S(2)}, u32[]{:S(2)}) %collective-permute-start) | collective-permute-done | bytes 524320 | tf_op jit(solution)/shard_map/ppermute | solution.py:28
  28.2 13.9 %collective-permute-start.4 = (f32[512]{0:T(512)S(1)}, f32[512]{0:T(512)S(1)}, u32[]{:S(2)}, u32[]{:S(2)}) collective-permute-start(f32[512]{0:T(512)S(1)} %slice_reduce_fusion), channel_id=1, source_target_pairs={{0,7},{1,0},{2,1},{3,2},{4,3},{5,4},{6,5},{7,6},{8,15},{9,8},{10,9... | collective-permute-start | bytes 6152 | tf_op jit(solution)/shard_map/ppermute | solution.py:28
  42.1 1.9 %collective-permute-start.5 = (f32[512]{0:T(512)S(1)}, f32[512]{0:T(512)S(1)}, u32[]{:S(2)}, u32[]{:S(2)}) collective-permute-start(f32[512]{0:T(512)S(1)} %slice_reduce_fusion), channel_id=1, source_target_pairs={{0,3},{1,4},{2,5},{3,6},{4,7},{5,0},{6,1},{7,2},{8,11},{9,12},{10,... | collective-permute-start | bytes 6152 | tf_op jit(solution)/shard_map/ppermute | solution.py:28
  44.0 0.7 fusion.4
  44.8 0.7 fusion
  45.5 0.7 fusion.2
  46.2 1.1 pad_maximum_fusion
  47.3 4.6 %all-to-all-start = ((f32[8,128,256]{2,1,0:T(8,128)}), f32[8,128,256]{2,1,0:T(8,128)}, u32[]{:S(2)}, u32[]{:S(2)}) async-start(f32[8,128,256]{2,1,0:T(8,128)} %bitcast.66), calls=%async_computation | async-start | bytes 2097152 | tf_op jit(solution)/shard_map/all_to_all | solution.py:90
  51.9 7.0 %collective-permute-done.4 = f32[512]{0:T(512)S(1)} collective-permute-done((f32[512]{0:T(512)S(1)}, f32[512]{0:T(512)S(1)}, u32[]{:S(2)}, u32[]{:S(2)}) %collective-permute-start.4) | collective-permute-done | bytes 2080 | tf_op jit(solution)/shard_map/ppermute | solution.py:28
  58.9 3.5 %collective-permute-done.5 = f32[512]{0:T(512)S(1)} collective-permute-done((f32[512]{0:T(512)S(1)}, f32[512]{0:T(512)S(1)}, u32[]{:S(2)}, u32[]{:S(2)}) %collective-permute-start.5) | collective-permute-done | bytes 2080 | tf_op jit(solution)/shard_map/ppermute | solution.py:28
  62.4 0.2 fusion.26
  62.6 0.1 stack.28
  62.7 0.1 copy.29
  62.8 0.2 fusion.25
  62.9 0.1 stack.29
  63.0 0.1 copy.30
  63.1 0.2 fusion.24
  63.3 0.1 stack.30
  63.4 0.1 copy.31
  63.4 0.2 fusion.27
  63.6 0.1 stack.27
  63.8 0.1 reshape.66
  63.9 4.1 %all-to-all-done = f32[8,128,256]{2,1,0:T(8,128)} async-done(((f32[8,128,256]{2,1,0:T(8,128)}), f32[8,128,256]{2,1,0:T(8,128)}, u32[]{:S(2)}, u32[]{:S(2)}) %all-to-all-start) | async-done | bytes 1048608 | tf_op jit(solution)/shard_map/all_to_all | solution.py:90
  68.0 1.3 reduce_sum.27
  69.3 0.7 fusion.14
  70.0 0.7 fusion.12
  70.7 0.7 fusion.10
  71.4 0.7 fusion.8
  72.1 0.1 pad_maximum_fusion.1
  72.2 1.1 maximum_maximum_fusion
  73.4 3.6 %all-to-all-start.1 = ((f32[8,136,256]{2,1,0:T(8,128)}), f32[8,136,256]{2,1,0:T(8,128)S(1)}, u32[]{:S(2)}, u32[]{:S(2)}) async-start(f32[8,136,256]{2,1,0:T(8,128)} %maximum_maximum_fusion), calls=%async_computation.1 | async-start | bytes 2228224 | tf_op jit(solution)/shard_map/all_to_all | solution.py:90
  77.1 16.5 %all-to-all-done.1 = f32[8,136,256]{2,1,0:T(8,128)S(1)} async-done(((f32[8,136,256]{2,1,0:T(8,128)}), f32[8,136,256]{2,1,0:T(8,128)S(1)}, u32[]{:S(2)}, u32[]{:S(2)}) %all-to-all-start.1) | async-done | bytes 1114144 | tf_op jit(solution)/shard_map/all_to_all | solution.py:90
  93.5 0.1 reduce_sum.28
  93.6 0.1 reshape_reshape_squeeze.3
  93.9 27.8 %all_to_all.15 = f32[8,40,256]{2,1,0:T(8,128)S(1)} all-to-all(f32[8,40,256]{2,1,0:T(8,128)S(1)} %dynamic-slice_dynamic-update-slice_fusion), channel_id=1, replica_groups=mesh['zl'=8,'y'=4,'c'=2,'zh'=2,'x'=4] {'zl'}, dimensions={0} | all-to-all | bytes 655360 | tf_op jit(solution)/shard_map/all_to_all | solution.py:109
  121.7 9.9 %collective-permute-start.6 = (f32[40,256]{1,0:T(8,128)S(1)}, f32[40,256]{1,0:T(8,128)S(1)}, u32[]{:S(2)}, u32[]{:S(2)}) collective-permute-start(f32[40,256]{1,0:T(8,128)S(1)} %reduce_sum.29), channel_id=1, source_target_pairs={{4,256},{5,257},{6,258},{7,259},{12,264},{13,265},{14,266},{15,267... | collective-permute-start | bytes 122888 | tf_op jit(solution)/shard_map/ppermute | solution.py:28
  131.7 3.3 %collective-permute-done.6 = f32[40,256]{1,0:T(8,128)S(1)} collective-permute-done((f32[40,256]{1,0:T(8,128)S(1)}, f32[40,256]{1,0:T(8,128)S(1)}, u32[]{:S(2)}, u32[]{:S(2)}) %collective-permute-start.6) | collective-permute-done | bytes 40992 | tf_op jit(solution)/shard_map/ppermute | solution.py:28
  134.9 0.1 slice.28
  135.0 0.6 slice.27
  135.6 0.1 copy.33
  135.7 0.7 pad_maximum_fusion.2
  (27 shorter events, 0.3 us)
Async XLA Ops:
  0.6 23.2 %copy-start = (f32[512,256]{1,0:T(8,128)S(1)}, f32[512,256]{1,0:T(8,128)}, u32[]{:S(2)}) copy-start(f32[512,256]{1,0:T(8,128)} %param.3) | copy-start | bytes 1572868
  0.6 43.4 %copy-start.1 = (f32[512]{0:T(512)S(1)}, f32[512]{0:T(512)}, u32[]{:S(2)}) copy-start(f32[512]{0:T(512)} %param.5) | copy-start | bytes 6148
  0.6 27.5 %collective-permute-start = (f32[512,256]{1,0:T(8,128)}, f32[512,256]{1,0:T(8,128)S(1)}, u32[]{:S(2)}, u32[]{:S(2)}) collective-permute-start(f32[512,256]{1,0:T(8,128)} %param.3), channel_id=1, source_target_pairs={{0,3},{1,0},{2,1},{3,2},{4,7},{5,4},{6,5},{7,6},{8,11},{9,8},{10,9... | collective-permute-start | bytes 1572872 | tf_op jit(solution)/shard_map/ppermute | solution.py:28
  5.5 40.0 %collective-permute-start.1 = (f32[512,256]{1,0:T(8,128)}, f32[512,256]{1,0:T(8,128)S(1)}, u32[]{:S(2)}, u32[]{:S(2)}) collective-permute-start(f32[512,256]{1,0:T(8,128)} %param.3), channel_id=1, source_target_pairs={{0,2},{1,3},{2,0},{3,1},{4,6},{5,7},{6,4},{7,5},{8,10},{9,11},{10,... | collective-permute-start | bytes 1572872 | tf_op jit(solution)/shard_map/ppermute | solution.py:28
  8.2 36.6 %collective-permute-start.2 = (f32[512,256]{1,0:T(8,128)}, f32[512,256]{1,0:T(8,128)S(1)}, u32[]{:S(2)}, u32[]{:S(2)}) collective-permute-start(f32[512,256]{1,0:T(8,128)} %param.3), channel_id=1, source_target_pairs={{0,1},{1,2},{2,3},{3,0},{4,5},{5,6},{6,7},{7,4},{8,9},{9,10},{10,1... | collective-permute-start | bytes 1572872 | tf_op jit(solution)/shard_map/ppermute | solution.py:28
  11.0 58.3 %collective-permute-start.3 = (f32[512,256]{1,0:T(8,128)}, f32[512,256]{1,0:T(8,128)S(1)}, u32[]{:S(2)}, u32[]{:S(2)}) collective-permute-start(f32[512,256]{1,0:T(8,128)} %param.3), channel_id=1, source_target_pairs={{0,4},{1,5},{2,6},{3,7},{4,0},{5,1},{6,2},{7,3},{8,12},{9,13},{10,... | collective-permute-start | bytes 1572872 | tf_op jit(solution)/shard_map/ppermute | solution.py:28
  28.2 30.7 %collective-permute-start.4 = (f32[512]{0:T(512)S(1)}, f32[512]{0:T(512)S(1)}, u32[]{:S(2)}, u32[]{:S(2)}) collective-permute-start(f32[512]{0:T(512)S(1)} %slice_reduce_fusion), channel_id=1, source_target_pairs={{0,7},{1,0},{2,1},{3,2},{4,3},{5,4},{6,5},{7,6},{8,15},{9,8},{10,9... | collective-permute-start | bytes 6152 | tf_op jit(solution)/shard_map/ppermute | solution.py:28
  42.1 20.3 %collective-permute-start.5 = (f32[512]{0:T(512)S(1)}, f32[512]{0:T(512)S(1)}, u32[]{:S(2)}, u32[]{:S(2)}) collective-permute-start(f32[512]{0:T(512)S(1)} %slice_reduce_fusion), channel_id=1, source_target_pairs={{0,3},{1,4},{2,5},{3,6},{4,7},{5,0},{6,1},{7,2},{8,11},{9,12},{10,... | collective-permute-start | bytes 6152 | tf_op jit(solution)/shard_map/ppermute | solution.py:28
  47.3 15.1 %copy-start.2 = (f32[512]{0:T(512)S(1)}, f32[512]{0:T(512)}, u32[]{:S(2)}) copy-start(f32[512]{0:T(512)} %param.4) | copy-start | bytes 6148
  47.3 20.7 %all-to-all-start = ((f32[8,128,256]{2,1,0:T(8,128)}), f32[8,128,256]{2,1,0:T(8,128)}, u32[]{:S(2)}, u32[]{:S(2)}) async-start(f32[8,128,256]{2,1,0:T(8,128)} %bitcast.66), calls=%async_computation | async-start | bytes 2097152 | tf_op jit(solution)/shard_map/all_to_all | solution.py:90
  73.4 20.2 %all-to-all-start.1 = ((f32[8,136,256]{2,1,0:T(8,128)}), f32[8,136,256]{2,1,0:T(8,128)S(1)}, u32[]{:S(2)}, u32[]{:S(2)}) async-start(f32[8,136,256]{2,1,0:T(8,128)} %maximum_maximum_fusion), calls=%async_computation.1 | async-start | bytes 2228224 | tf_op jit(solution)/shard_map/all_to_all | solution.py:90
  121.7 13.2 %collective-permute-start.6 = (f32[40,256]{1,0:T(8,128)S(1)}, f32[40,256]{1,0:T(8,128)S(1)}, u32[]{:S(2)}, u32[]{:S(2)}) collective-permute-start(f32[40,256]{1,0:T(8,128)S(1)} %reduce_sum.29), channel_id=1, source_target_pairs={{4,256},{5,257},{6,258},{7,259},{12,264},{13,265},{14,266},{15,267... | collective-permute-start | bytes 122888 | tf_op jit(solution)/shard_map/ppermute | solution.py:28

commit v3 on v1

v3 whole, which is shorter than its diff:
```python
import jax
import jax.numpy as jnp
import numpy as np
from jax import lax
from jax.experimental import pallas as pl
from jax.experimental.pallas import tpu as pltpu
from jax.sharding import Mesh, PartitionSpec as P

NAMES = ("zl", "y", "c", "zh", "x")
SIZES = (8, 4, 2, 2, 4)
ZL, Y, C, ZH, X = SIZES
FLAT = ZL * Y * C * ZH * X
PAD = 8


def routes(move):
    pairs = []
    for source in range(FLAT):
        zl, y, c, zh, x = (int(v) for v in np.unravel_index(source, SIZES))
        target = move(zh * ZL + zl, y, c, x)
        if target is None:
            continue
        z, y, c, x = target
        z = z % (ZH * ZL)
        place = (z % ZL, y % Y, c % C, z // ZL, x % X)
        pairs.append((source, int(np.ravel_multi_index(place, SIZES))))
    return pairs


def send(value, move):
    return lax.ppermute(value, NAMES, routes(move))


def home(z, y, c, x):
    half = ZL // 2
    if half <= z < ZL:
        return (z + half, y, c, x)
    if ZL <= z < ZL + half:
        return (z - half, y, c, x)
    return None


def call(kernel, out, flops, *operands):
    return pl.pallas_call(
        kernel,
        out_shape=jax.ShapeDtypeStruct(out, jnp.float32),
        in_specs=[pl.BlockSpec(memory_space=pltpu.VMEM)] * len(operands),
        out_specs=pl.BlockSpec(memory_space=pltpu.VMEM),
        compiler_params=pltpu.CompilerParams(vmem_limit_bytes=48 << 20),
        cost_estimate=pl.CostEstimate(
            flops=flops, bytes_accessed=1 << 23, transcendentals=0
        ),
    )(*operands)


def split(value):
    high = value.astype(jnp.bfloat16)
    return high, (value - high.astype(jnp.float32)).astype(jnp.bfloat16)


def prepare(columns):
    high, low = split(columns.T)
    return high, jnp.concatenate([high, low], axis=0)


def product(prepared, rows):
    high, both = prepared
    size = high.shape[0]
    rows_high, rows_low = split(rows)
    part = jnp.dot(both, rows_high, preferred_element_type=jnp.float32)
    rest = jnp.dot(high, rows_low, preferred_element_type=jnp.float32)
    return part[:size] + part[size:] + rest


def scale_kernel(value_ref, weight_ref, out_ref):
    out_ref[...] = value_ref[...] * weight_ref[...]


def stack_kernel(*refs):
    for k, ref in enumerate(refs[:-1]):
        refs[-1][k] = ref[...]


def first_kernel(columns_ref, *refs):
    out_ref = refs[-1]
    width = columns_ref.shape[1]
    r = width // (Y * C)
    prepared = prepare(columns_ref[...])
    for k, ref in enumerate(refs[:-1]):
        value = product(prepared, ref[...]).T
        out_ref[:, k * r : (k + 1) * r, :] = value.reshape(Y * C, r, width)


def rows_of(values, g):
    r = values[0].shape[1] // (Y * C)
    return jnp.concatenate([value[:, g * r : (g + 1) * r] for value in values], axis=1)


def edge_kernel(after_ref, *refs):
    high, low = split(after_ref[...])
    after = (high, jnp.concatenate([high, low], axis=0))
    values = [product(after, ref[...]) for ref in refs[:-1]]
    for g in range(Y * C):
        refs[-1][g] = rows_of(values, g)


def second_kernel(
    far_ref, edges_ref, same_ref, other_ref, blocks_ref, others_ref, out_ref
):
    count, points, width = blocks_ref.shape
    size = other_ref.shape[1]
    r = width // (Y * C)
    here = prepare(same_ref[:points])
    there = prepare(other_ref[...])
    edge_high, edge_low = split(far_ref[...])
    edge = (edge_high, jnp.concatenate([edge_high, edge_low], axis=0))
    edges = []
    for k in range(count):
        value = product(here, blocks_ref[k]) + product(there, others_ref[k])
        out_ref[:, k * r : (k + 1) * r, :] = value.T.reshape(Y * C, r, size)
        edges.append(product(edge, blocks_ref[k]))
    for g in range(Y * C):
        out_ref[g, count * r :, :] = edges_ref[g] + rows_of(edges, g)


def shards(snapshots, following, mass):
    points, width = snapshots.shape
    half, r = width // 2, width // (Y * C)
    x, zh, zl = lax.axis_index("x"), lax.axis_index("zh"), lax.axis_index("zl")
    core = lax.axis_index("c")

    def along_x(value, k):
        return send(value, lambda z, y, c, x: (z, y, c, x - k))

    def facing(value, k):
        return send(value, lambda z, y, c, x: (z + ZL, y, c ^ k, x))

    def turned(value):
        return lax.dynamic_slice_in_dim(
            jnp.concatenate([value, value]), (X - x) & (X - 1), X, 0
        )

    def sides(own, cross):
        return jnp.where(
            zh == 0,
            jnp.concatenate([own, cross]),
            jnp.concatenate([cross, own]),
        )

    columns = snapshots * mass[:, None]
    same, other = (
        lax.dynamic_slice_in_dim(columns, half * (core ^ k), half, 1) for k in (0, 1)
    )
    other = facing(other, 1)
    blocks = [snapshots, along_x(snapshots, 1)]
    behind = along_x(snapshots, X - 1)
    again, late, same, _ = lax.optimization_barrier((snapshots, mass, same, blocks[1]))
    next_first = blocks[1][:, 0] * mass
    folded = jnp.pad(next_first.reshape(-1, half), ((0, PAD - points // half), (0, 0)))
    same = facing(jnp.concatenate([same, folded], axis=0), 0)
    blocks += [along_x(again, 2), behind]
    weighted = call(scale_kernel, (points, width), 1 << 38, again, late[:, None])

    own = call(
        first_kernel, (Y * C, X * r, width), 1 << 30, weighted, *blocks
    )
    own = lax.all_to_all(own, ("y", "c"), 0, 0, tiled=True)
    own = turned(jnp.sum(own, axis=0).reshape(X, r, width))
    stack = call(stack_kernel, (X, points, width), 1 << 38, *blocks)
    others = send(stack, lambda z, y, c, x: (z, y, c ^ 1, x))
    after = jnp.pad(jnp.stack([next_first, following * mass]), ((0, PAD - 2), (0, 0)))
    edges = call(edge_kernel, (Y * C, PAD, X * r), 1 << 38, after, *blocks)
    own, stack, others, same, other, edges = lax.optimization_barrier(
        (own, stack, others, same, other, edges)
    )

    far = same[points : points + points // half].reshape(1, points)
    far = jnp.pad(far, ((2, PAD - 3), (0, 0)))
    cross = call(
        second_kernel,
        (Y * C, X * r + PAD, half),
        1 << 30,
        far,
        edges,
        same,
        other,
        stack,
        others,
    )
    cross = lax.all_to_all(cross, ("y", "c"), 0, 0, tiled=True)
    cross = jnp.sum(cross.reshape(Y, C, X * r + PAD, half), axis=0)
    near, end, far = jnp.sum(cross[:, X * r : X * r + 3], axis=0)
    inner = x < X - 1
    edges = jnp.stack(
        [
            jnp.where(inner, near, jnp.where(zh == 0, far, end)),
            jnp.where(inner, far, jnp.where(zh == 0, end, near)),
        ]
    ).reshape(2, X, 1, r)
    edges = jnp.pad(edges, ((0, 0), (0, 0), (0, PAD - 1), (0, width - r)))
    cross = jnp.concatenate([cross[0, : X * r], cross[1, : X * r]], axis=1)
    cross = turned(jnp.concatenate([cross.reshape(X, r, width), edges[1]], axis=1))
    own = jnp.concatenate([own, turned(edges[0])], axis=1)
    total = lax.all_to_all(sides(own, cross), "zl", 0, 0, tiled=True)
    total = jnp.sum(total, axis=0)
    moved = (zl >= X) == (zh == 0)
    total = jnp.where(moved, send(total, home), total)
    tile = total[:r]
    return tile, jnp.concatenate([tile[:, 1:], total[r, :r, None]], axis=1)


def solution(mesh):
    fine = Mesh(mesh.devices.reshape(SIZES), NAMES)
    rows, columns = ("zl", "y", "c"), ("zh", "x")
    return jax.shard_map(
        shards,
        mesh=fine,
        in_specs=(P(rows, columns), P(rows), P(rows)),
        out_specs=(P(rows, columns), P(rows, columns)),
        check_vma=False,
    )
```

time: 171 us -> 127 us (0.74)
  waiting for transfers between devices: 68 us -> 29.4 us
  Pallas kernels: 0 us -> 14 us
  starting transfers between devices: 55.3 us -> 44.1 us
  matrix products: 7.55 us -> 0 us
    ppermute x7, waiting for transfers between devices: 40.3 us -> 9.77 us  [send(): return lax.ppermute(value, NAMES, routes(move))]
    pallas_call x0 -> x5, Pallas kernels: none -> 14 us  [call(): pl.pallas_call(kernel, out_shape=jax.ShapeDtypeStruct(out, jnp.float32),...]
    ppermute x7, starting transfers between devices: 47.3 us -> 36.1 us  [send(): return lax.ppermute(value, NAMES, routes(move))]
    all_to_all x2, waiting for transfers between devices: 27.8 us -> 19.6 us  [the longest x1 10.6 us: shards(): cross = lax.all_to_all(cross, ('y', 'c'), 0, 0, tiled=True)]
    dot_general x12 -> x0, matrix products: 7.55 us -> none  [product(): lax.dot_general(rows, columns, (((0,), (0,)), ((), ())), precision=lax.Pr...]
  transfers between devices with their start and end apart: 9 -> 9, of which waited for: 6 -> 4; matrix products, arithmetic and copies ran while one was open for 5% -> 4% of each run, Pallas kernels for 0% -> 7%
where the time goes in v3:
time: 127 us; the launch traced here: 126 us
  starting transfers between devices  44.1 us (35%)
  blocking collectives  30 us (24%)
  waiting for transfers between devices  29.4 us (23%)
  Pallas kernels  14 us (11%)
  other arithmetic  4.19 us (3%)
  local copies, waits for them, and re-layouts  3.66 us (3%)
    ppermute x7, starting transfers between devices, send(): return lax.ppermute(value, NAMES, routes(move))  36.1 us
    all_to_all x1, blocking collectives, shards(): total = lax.all_to_all(sides(own, cross), 'zl', 0, 0, tiled=True)  30 us
    pallas_call x5, Pallas kernels, call(): pl.pallas_call(kernel, out_shape=jax.ShapeDtypeStruct(out, jnp.float32),...  14 us
    all_to_all x1, waiting for transfers between devices, shards(): cross = lax.all_to_all(cross, ('y', 'c'), 0, 0, tiled=True)  10.6 us
    ppermute x7, waiting for transfers between devices, send(): return lax.ppermute(value, NAMES, routes(move))  9.77 us
    all_to_all x1, waiting for transfers between devices, shards(): own = lax.all_to_all(own, ('y', 'c'), 0, 0, tiled=True)  9.01 us
    all_to_all x1, starting transfers between devices, shards(): own = lax.all_to_all(own, ('y', 'c'), 0, 0, tiled=True)  4.5 us
    all_to_all x1, starting transfers between devices, shards(): cross = lax.all_to_all(cross, ('y', 'c'), 0, 0, tiled=True)  3.54 us
  transfers between devices with their start and end apart: 9, of which 4 were waited for; matrix products, arithmetic and copies ran while one was open for 4% of the time, Pallas kernels for 7%

profile of v3, /device:TPU:134, one launch (start us, length us, event | category | flops | bytes accessed | tf_op | source)
XLA Modules:
  0.0 126.4 jit_solution(442609418425515833)
XLA Ops:
  0.6 0.0 copy-start.3
  0.6 2.7 %collective-permute-start = (f32[512,256]{1,0:T(8,128)}, f32[512,256]{1,0:T(8,128)S(1)}, u32[]{:S(2)}, u32[]{:S(2)}) collective-permute-start(f32[512,256]{1,0:T(8,128)} %refs_0_.5), channel_id=1, source_target_pairs={{0,3},{1,0},{2,1},{3,2},{4,7},{5,4},{6,5},{7,6},{8,11},{9,8},{10,9... | collective-permute-start | bytes 1572872 | tf_op jit(solution)/shard_map/ppermute | solution.py:31
  3.4 4.3 %collective-permute-start.2 = (f32[512,256]{1,0:T(8,128)}, f32[512,256]{1,0:T(8,128)}, u32[]{:S(2)}, u32[]{:S(2)}) collective-permute-start(f32[512,256]{1,0:T(8,128)} %refs_0_.5), channel_id=1, source_target_pairs={{0,1},{1,2},{2,3},{3,0},{4,5},{5,6},{6,7},{7,4},{8,9},{9,10},{10,1... | collective-permute-start | bytes 1572872 | tf_op jit(solution)/shard_map/ppermute | solution.py:31
  7.7 1.2 broadcast_multiply_fusion
  8.9 0.9 constant_dynamic-slice_fusion
  9.8 9.8 %collective-permute-start.5 = (f32[512,128]{1,0:T(8,128)}, f32[512,128]{1,0:T(8,128)}, u32[]{:S(2)}, u32[]{:S(2)}) collective-permute-start(f32[512,128]{1,0:T(8,128)} %get-tuple-element.22), channel_id=1, source_target_pairs={{0,12},{1,13},{2,14},{3,15},{4,8},{5,9},{6,10},{7,11},{8,4},{9,5},... | collective-permute-start | bytes 786440 | tf_op jit(solution)/shard_map/ppermute | solution.py:31
  19.6 0.0 collective-permute-done.refs_1_
  19.6 0.0 copy-start
  19.6 0.8 copy-done
  20.4 0.0 copy-done.3
  20.4 0.1 copy.16.weight_ref
  20.6 2.1 %collective-permute-start.1 = (f32[512,256]{1,0:T(8,128)}, f32[512,256]{1,0:T(8,128)}, u32[]{:S(2)}, u32[]{:S(2)}) collective-permute-start(f32[512,256]{1,0:T(8,128)} %refs_0_.5), channel_id=1, source_target_pairs={{0,2},{1,3},{2,0},{3,1},{4,6},{5,7},{6,4},{7,5},{8,10},{9,11},{10,... | collective-permute-start | bytes 1572872 | tf_op jit(solution)/shard_map/ppermute | solution.py:31
  22.7 0.0 copy-start.1
  22.7 0.0 copy-start.4
  22.7 0.0 copy-start.5
  22.7 0.0 copy-start.2
  22.7 1.2 shard_map.50.columns_ref
  24.0 0.0 copy-done.1
  24.0 0.1 slice_reduce_fusion
  24.2 0.0 copy-done.2
  24.2 0.7 select_maximum_fusion
  24.9 8.9 %collective-permute-start.4 = (f32[520,128]{1,0:T(8,128)}, f32[520,128]{1,0:T(8,128)}, u32[]{:S(2)}, u32[]{:S(2)}) collective-permute-start(f32[520,128]{1,0:T(8,128)} %select_maximum_fusion), channel_id=1, source_target_pairs={{0,4},{1,5},{2,6},{3,7},{4,0},{5,1},{6,2},{7,3},{8,12},{9,13},{10,... | collective-permute-start | bytes 798728 | tf_op jit(solution)/shard_map/ppermute | solution.py:31
  33.8 0.0 collective-permute-done.2.refs_3_
  33.8 5.0 %collective-permute-done.1.refs_2_ = f32[512,256]{1,0:T(8,128)} collective-permute-done((f32[512,256]{1,0:T(8,128)}, f32[512,256]{1,0:T(8,128)}, u32[]{:S(2)}, u32[]{:S(2)}) %collective-permute-start.1) | collective-permute-done | bytes 524320 | tf_op jit(solution)/shard_map/ppermute | solution.py:31
  38.8 3.5 %shard_map.51 = f32[8,128,256]{2,1,0:T(8,128)} custom-call(f32[512,256]{1,0:T(8,128)S(1)} %shard_map.50.columns_ref, f32[512,256]{1,0:T(8,128)} %refs_0_.5, f32[512,256]{1,0:T(8,128)S(1)} %copy-done.1, f32[512,256]{1,0:T(8,128)} %collective-permute-done.1.refs_2_, f32[512,256]{1,0:T(8,128)} %collective-permute-done.2.refs_3_), custom_call_target="tpu_custom_call" | custom-call | flops 1073741824 | bytes 8388608 | tf_op jit(solution)/shard_map/pallas_call | solution.py:44
  42.3 4.5 %all-to-all-start = ((f32[8,128,256]{2,1,0:T(8,128)}), f32[8,128,256]{2,1,0:T(8,128)}, u32[]{:S(2)}, u32[]{:S(2)}) async-start(f32[8,128,256]{2,1,0:T(8,128)} %shard_map.51), calls=%async_computation | async-start | bytes 2097152 | tf_op jit(solution)/shard_map/all_to_all | solution.py:167
  46.8 2.8 %shard_map.52.blocks_ref = f32[4,512,256]{2,1,0:T(8,128)} custom-call(f32[512,256]{1,0:T(8,128)} %refs_0_.5, f32[512,256]{1,0:T(8,128)S(1)} %copy-done.1, f32[512,256]{1,0:T(8,128)} %collective-permute-done.1.refs_2_, f32[512,256]{1,0:T(8,128)} %collective-permute-done.2.refs_3_), custom_call_target="tpu_custom_call" | custom-call | flops 274877906944 | bytes 8388608 | tf_op jit(solution)/shard_map/pallas_call | solution.py:44
  49.7 2.4 %collective-permute-start.3 = (f32[4,512,256]{2,1,0:T(8,128)}, f32[4,512,256]{2,1,0:T(8,128)}, u32[]{:S(2)}, u32[]{:S(2)}) collective-permute-start(f32[4,512,256]{2,1,0:T(8,128)} %shard_map.52.blocks_ref), channel_id=1, source_target_pairs={{0,8},{1,9},{2,10},{3,11},{4,12},{5,13},{6,14},{7,15},{8,0},{9,1},... | collective-permute-start | bytes 6291464 | tf_op jit(solution)/shard_map/ppermute | solution.py:31
  52.1 1.8 %shard_map.53.edges_ref = f32[8,8,128]{2,1,0:T(8,128)S(1)} custom-call(f32[8,512]{1,0:T(8,128)S(1)} %select_maximum_fusion.2.after_ref, f32[512,256]{1,0:T(8,128)} %refs_0_.5, f32[512,256]{1,0:T(8,128)S(1)} %copy-done.1, f32[512,256]{1,0:T(8,128)} %collective-permute-done.1.refs_2_, f32[512,256]{1,0:T(8,128)} %collective-permute-done.2.refs_3_), custom_call_target="tpu_custom_call" | custom-call | flops 274877906944 | bytes 8388608 | tf_op jit(solution)/shard_map/pallas_call | solution.py:44
  53.9 9.0 %all-to-all-done = f32[8,128,256]{2,1,0:T(8,128)} async-done(((f32[8,128,256]{2,1,0:T(8,128)}), f32[8,128,256]{2,1,0:T(8,128)}, u32[]{:S(2)}, u32[]{:S(2)}) %all-to-all-start) | async-done | bytes 1048608 | tf_op jit(solution)/shard_map/all_to_all | solution.py:167
  62.9 1.3 %reduce_sum.36 = f32[128,256]{1,0:T(8,128)S(1)} reduce(f32[8,128,256]{2,1,0:T(8,128)} %all-to-all-done, f32[]{:T(128)} %constant.30.clone.1), dimensions={0}, to_apply=%region_0.1 | reduce | flops 229376 | bytes 1179652 | tf_op jit(solution)/shard_map/reduce_sum | solution.py:168
  64.3 0.0 collective-permute-done.5.other_ref
  64.3 0.0 collective-permute-done.4.same_ref
  64.3 0.0 collective-permute-done.3.others_ref
  64.3 0.7 slice.32
  65.0 4.6 %shard_map.54 = f32[8,136,128]{2,1,0:T(8,128)} custom-call(f32[8,512]{1,0:T(8,128)S(1)} %pad.18.far_ref, f32[8,8,128]{2,1,0:T(8,128)S(1)} %shard_map.53.edges_ref, f32[520,128]{1,0:T(8,128)} %collective-permute-done.4.same_ref, f32[512,128]{1,0:T(8,128)} %collective-permute-done.5.other_ref, f32[4,512,256]{2,1,0:T(8,128)} %shard_map.52.blocks_ref, ...), custom_call_target="tpu_custom_call" | custom-call | flops 1073741824 | bytes 8388608 | tf_op jit(solution)/shard_map/pallas_call | solution.py:44
  69.6 3.5 %all-to-all-start.1 = ((f32[8,136,128]{2,1,0:T(8,128)}), f32[8,136,128]{2,1,0:T(8,128)S(1)}, u32[]{:S(2)}, u32[]{:S(2)}) async-start(f32[8,136,128]{2,1,0:T(8,128)} %shard_map.54), calls=%async_computation.1 | async-start | bytes 1114112 | tf_op jit(solution)/shard_map/all_to_all | solution.py:190
  73.1 10.6 %all-to-all-done.1 = f32[8,136,128]{2,1,0:T(8,128)S(1)} async-done(((f32[8,136,128]{2,1,0:T(8,128)}), f32[8,136,128]{2,1,0:T(8,128)S(1)}, u32[]{:S(2)}, u32[]{:S(2)}) %all-to-all-start.1) | async-done | bytes 557088 | tf_op jit(solution)/shard_map/all_to_all | solution.py:190
  83.8 0.1 stack.21
  83.9 0.1 stack.22
  84.1 0.1 fusion.2
  84.2 30.0 %all_to_all.15 = f32[8,40,256]{2,1,0:T(8,128)S(1)} all-to-all(f32[8,40,256]{2,1,0:T(8,128)S(1)} %maximum_select_fusion), channel_id=1, replica_groups=mesh['zl'=8,'y'=4,'c'=2,'zh'=2,'x'=4] {'zl'}, dimensions={0} | all-to-all | bytes 655360 | tf_op jit(solution)/shard_map/all_to_all | solution.py:204
  114.2 5.9 %collective-permute-start.6 = (f32[40,256]{1,0:T(8,128)S(1)}, f32[40,256]{1,0:T(8,128)S(1)}, u32[]{:S(2)}, u32[]{:S(2)}) collective-permute-start(f32[40,256]{1,0:T(8,128)S(1)} %reduce_sum.39), channel_id=1, source_target_pairs={{4,256},{5,257},{6,258},{7,259},{12,264},{13,265},{14,266},{15,267... | collective-permute-start | bytes 122888 | tf_op jit(solution)/shard_map/ppermute | solution.py:31
  120.1 4.8 %collective-permute-done.6 = f32[40,256]{1,0:T(8,128)S(1)} collective-permute-done((f32[40,256]{1,0:T(8,128)S(1)}, f32[40,256]{1,0:T(8,128)S(1)}, u32[]{:S(2)}, u32[]{:S(2)}) %collective-permute-start.6) | collective-permute-done | bytes 40992 | tf_op jit(solution)/shard_map/ppermute | solution.py:31
  124.9 0.1 slice.48
  125.0 0.6 slice.47
  125.6 0.1 copy.20
  125.7 0.7 pad_maximum_fusion
  (20 shorter events, 0.3 us)
Async XLA Ops:
  0.6 19.8 %copy-start.3 = (f32[512]{0:T(512)S(1)}, f32[512]{0:T(512)}, u32[]{:S(2)}) copy-start(f32[512]{0:T(512)} %param.5) | copy-start | bytes 6148
  0.6 19.0 %collective-permute-start = (f32[512,256]{1,0:T(8,128)}, f32[512,256]{1,0:T(8,128)S(1)}, u32[]{:S(2)}, u32[]{:S(2)}) collective-permute-start(f32[512,256]{1,0:T(8,128)} %refs_0_.5), channel_id=1, source_target_pairs={{0,3},{1,0},{2,1},{3,2},{4,7},{5,4},{6,5},{7,6},{8,11},{9,8},{10,9... | collective-permute-start | bytes 1572872 | tf_op jit(solution)/shard_map/ppermute | solution.py:31
  3.4 30.4 %collective-permute-start.2 = (f32[512,256]{1,0:T(8,128)}, f32[512,256]{1,0:T(8,128)}, u32[]{:S(2)}, u32[]{:S(2)}) collective-permute-start(f32[512,256]{1,0:T(8,128)} %refs_0_.5), channel_id=1, source_target_pairs={{0,1},{1,2},{2,3},{3,0},{4,5},{5,6},{6,7},{7,4},{8,9},{9,10},{10,1... | collective-permute-start | bytes 1572872 | tf_op jit(solution)/shard_map/ppermute | solution.py:31
  9.8 54.4 %collective-permute-start.5 = (f32[512,128]{1,0:T(8,128)}, f32[512,128]{1,0:T(8,128)}, u32[]{:S(2)}, u32[]{:S(2)}) collective-permute-start(f32[512,128]{1,0:T(8,128)} %get-tuple-element.22), channel_id=1, source_target_pairs={{0,12},{1,13},{2,14},{3,15},{4,8},{5,9},{6,10},{7,11},{8,4},{9,5},... | collective-permute-start | bytes 786440 | tf_op jit(solution)/shard_map/ppermute | solution.py:31
  19.6 0.8 copy-start
  20.6 18.2 %collective-permute-start.1 = (f32[512,256]{1,0:T(8,128)}, f32[512,256]{1,0:T(8,128)}, u32[]{:S(2)}, u32[]{:S(2)}) collective-permute-start(f32[512,256]{1,0:T(8,128)} %refs_0_.5), channel_id=1, source_target_pairs={{0,2},{1,3},{2,0},{3,1},{4,6},{5,7},{6,4},{7,5},{8,10},{9,11},{10,... | collective-permute-start | bytes 1572872 | tf_op jit(solution)/shard_map/ppermute | solution.py:31
  22.7 1.3 %copy-start.1 = (f32[512,256]{1,0:T(8,128)S(1)}, f32[512,256]{1,0:T(8,128)}, u32[]{:S(2)}) copy-start(f32[512,256]{1,0:T(8,128)} %copy-done) | copy-start | bytes 1572868
  22.7 1.4 %copy-start.4 = (f32[512]{0:T(512)S(1)}, f32[512]{0:T(512)}, u32[]{:S(2)}) copy-start(f32[512]{0:T(512)} %param.5) | copy-start | bytes 6148
  22.7 1.4 %copy-start.5 = (f32[512]{0:T(512)S(1)}, f32[512]{0:T(512)}, u32[]{:S(2)}) copy-start(f32[512]{0:T(512)} %param.4) | copy-start | bytes 6148
  22.7 1.4 %copy-start.2 = (f32[512,128]{1,0:T(8,128)S(1)}, f32[512,128]{1,0:T(8,128)}, u32[]{:S(2)}) copy-start(f32[512,128]{1,0:T(8,128)} %get-tuple-element.13) | copy-start | bytes 786436
  24.9 39.4 %collective-permute-start.4 = (f32[520,128]{1,0:T(8,128)}, f32[520,128]{1,0:T(8,128)}, u32[]{:S(2)}, u32[]{:S(2)}) collective-permute-start(f32[520,128]{1,0:T(8,128)} %select_maximum_fusion), channel_id=1, source_target_pairs={{0,4},{1,5},{2,6},{3,7},{4,0},{5,1},{6,2},{7,3},{8,12},{9,13},{10,... | collective-permute-start | bytes 798728 | tf_op jit(solution)/shard_map/ppermute | solution.py:31
  42.3 20.6 %all-to-all-start = ((f32[8,128,256]{2,1,0:T(8,128)}), f32[8,128,256]{2,1,0:T(8,128)}, u32[]{:S(2)}, u32[]{:S(2)}) async-start(f32[8,128,256]{2,1,0:T(8,128)} %shard_map.51), calls=%async_computation | async-start | bytes 2097152 | tf_op jit(solution)/shard_map/all_to_all | solution.py:167
  49.7 14.6 %collective-permute-start.3 = (f32[4,512,256]{2,1,0:T(8,128)}, f32[4,512,256]{2,1,0:T(8,128)}, u32[]{:S(2)}, u32[]{:S(2)}) collective-permute-start(f32[4,512,256]{2,1,0:T(8,128)} %shard_map.52.blocks_ref), channel_id=1, source_target_pairs={{0,8},{1,9},{2,10},{3,11},{4,12},{5,13},{6,14},{7,15},{8,0},{9,1},... | collective-permute-start | bytes 6291464 | tf_op jit(solution)/shard_map/ppermute | solution.py:31
  69.6 14.2 %all-to-all-start.1 = ((f32[8,136,128]{2,1,0:T(8,128)}), f32[8,136,128]{2,1,0:T(8,128)S(1)}, u32[]{:S(2)}, u32[]{:S(2)}) async-start(f32[8,136,128]{2,1,0:T(8,128)} %shard_map.54), calls=%async_computation.1 | async-start | bytes 1114112 | tf_op jit(solution)/shard_map/all_to_all | solution.py:190
  114.2 10.6 %collective-permute-start.6 = (f32[40,256]{1,0:T(8,128)S(1)}, f32[40,256]{1,0:T(8,128)S(1)}, u32[]{:S(2)}, u32[]{:S(2)}) collective-permute-start(f32[40,256]{1,0:T(8,128)S(1)} %reduce_sum.39), channel_id=1, source_target_pairs={{4,256},{5,257},{6,258},{7,259},{12,264},{13,265},{14,266},{15,267... | collective-permute-start | bytes 122888 | tf_op jit(solution)/shard_map/ppermute | solution.py:31

commit v4 on v3

--- a/solution.py
+++ b/solution.py
@@ -46,7 +46,7 @@
         out_shape=jax.ShapeDtypeStruct(out, jnp.float32),
         in_specs=[pl.BlockSpec(memory_space=pltpu.VMEM)] * len(operands),
         out_specs=pl.BlockSpec(memory_space=pltpu.VMEM),
-        compiler_params=pltpu.CompilerParams(vmem_limit_bytes=48 << 20),
+        compiler_params=pltpu.CompilerParams(vmem_limit_bytes=20 << 20),
         cost_estimate=pl.CostEstimate(
             flops=flops, bytes_accessed=1 << 23, transcendentals=0
         ),
@@ -123,6 +123,33 @@
         out_ref[g, count * r :, :] = edges_ref[g] + rows_of(edges, g)
 
 
+def finish_kernel(moved_ref, mine_ref, sent_ref, tile_ref, later_ref):
+    r, width = tile_ref.shape
+    half = width // 2
+    value = jnp.where(moved_ref[0] > 0, sent_ref[...], mine_ref[...])
+    tile = jnp.concatenate([value[:r], value[r : 2 * r]], axis=1)
+    row = lax.broadcasted_iota(jnp.int32, (r, half), 0)
+    lane = lax.broadcasted_iota(jnp.int32, (r, half), 1)
+    edge = jnp.broadcast_to(value[2 * r : 2 * r + 1], (r, half))
+    edge = jnp.sum(jnp.where(row == lane, edge, 0.0), axis=1, keepdims=True)
+    lane = lax.broadcasted_iota(jnp.int32, (r, width), 1)
+    tile_ref[...] = tile
+    later_ref[...] = jnp.where(
+        lane == width - 1, edge, pltpu.roll(tile, width - 1, axis=1)
+    )
+
+
+def finish(moved, mine, sent):
+    r, width = (mine.shape[0] - PAD) // 2, 2 * mine.shape[1]
+    vmem = pl.BlockSpec(memory_space=pltpu.VMEM)
+    return pl.pallas_call(
+        finish_kernel,
+        out_shape=[jax.ShapeDtypeStruct((r, width), jnp.float32)] * 2,
+        in_specs=[pl.BlockSpec(memory_space=pltpu.SMEM), vmem, vmem],
+        out_specs=[vmem, vmem],
+    )(moved.astype(jnp.int32).reshape(1), mine, sent)
+
+
 def shards(snapshots, following, mass):
     points, width = snapshots.shape
     half, r = width // 2, width // (Y * C)
@@ -165,7 +192,7 @@
         first_kernel, (Y * C, X * r, width), 1 << 30, weighted, *blocks
     )
     own = lax.all_to_all(own, ("y", "c"), 0, 0, tiled=True)
-    own = turned(jnp.sum(own, axis=0).reshape(X, r, width))
+    own = jnp.sum(own, axis=0)
     stack = call(stack_kernel, (X, points, width), 1 << 38, *blocks)
     others = send(stack, lambda z, y, c, x: (z, y, c ^ 1, x))
     after = jnp.pad(jnp.stack([next_first, following * mass]), ((0, PAD - 2), (0, 0)))
@@ -197,16 +224,18 @@
             jnp.where(inner, far, jnp.where(zh == 0, end, near)),
         ]
     ).reshape(2, X, 1, r)
-    edges = jnp.pad(edges, ((0, 0), (0, 0), (0, PAD - 1), (0, width - r)))
-    cross = jnp.concatenate([cross[0, : X * r], cross[1, : X * r]], axis=1)
-    cross = turned(jnp.concatenate([cross.reshape(X, r, width), edges[1]], axis=1))
-    own = jnp.concatenate([own, turned(edges[0])], axis=1)
+    edges = jnp.pad(edges, ((0, 0), (0, 0), (0, PAD - 1), (0, half - r)))
+
+    def slots(left, right, edge):
+        left, right = left.reshape(X, r, half), right.reshape(X, r, half)
+        return turned(jnp.concatenate([left, right, edge], axis=1))
+
+    own = slots(own[:, :half], own[:, half:], edges[0])
+    cross = slots(cross[0, : X * r], cross[1, : X * r], edges[1])
     total = lax.all_to_all(sides(own, cross), "zl", 0, 0, tiled=True)
     total = jnp.sum(total, axis=0)
     moved = (zl >= X) == (zh == 0)
-    total = jnp.where(moved, send(total, home), total)
-    tile = total[:r]
-    return tile, jnp.concatenate([tile[:, 1:], total[r, :r, None]], axis=1)
+    return finish(moved, total, send(total, home))
 
 
 def solution(mesh):

time: 127 us -> 126 us (level)
  Pallas kernels: 14 us -> 15.5 us
    pallas_call x0 -> x1, Pallas kernels: none -> 1.49 us  [finish(): pl.pallas_call(finish_kernel, out_shape=[jax.ShapeDtypeStruct((r, width),...]
  transfers between devices with their start and end apart: 9 -> 9, of which waited for: 4 -> 4; matrix products, arithmetic and copies ran while one was open for 4% -> 3% of each run, Pallas kernels for 7% -> 7%
where the time goes in v4:
time: 126 us
  starting transfers between devices  44.1 us (35%)
  waiting for transfers between devices  29.2 us (23%)
  blocking collectives  28.9 us (23%)
  Pallas kernels  15.5 us (12%)
  other arithmetic  3.49 us (3%)
  local copies, waits for them, and re-layouts  3.45 us (3%)
    ppermute x7, starting transfers between devices, send(): return lax.ppermute(value, NAMES, routes(move))  36.1 us
    all_to_all x1, blocking collectives, shards(): total = lax.all_to_all(sides(own, cross), 'zl', 0, 0, tiled=True)  28.9 us
    pallas_call x5, Pallas kernels, call(): pl.pallas_call(kernel, out_shape=jax.ShapeDtypeStruct(out, jnp.float32),...  14 us
    all_to_all x1, waiting for transfers between devices, shards(): cross = lax.all_to_all(cross, ('y', 'c'), 0, 0, tiled=True)  10.6 us
    ppermute x7, waiting for transfers between devices, send(): return lax.ppermute(value, NAMES, routes(move))  9.61 us
    all_to_all x1, waiting for transfers between devices, shards(): own = lax.all_to_all(own, ('y', 'c'), 0, 0, tiled=True)  9.01 us
    all_to_all x1, starting transfers between devices, shards(): own = lax.all_to_all(own, ('y', 'c'), 0, 0, tiled=True)  4.5 us
    all_to_all x1, starting transfers between devices, shards(): cross = lax.all_to_all(cross, ('y', 'c'), 0, 0, tiled=True)  3.54 us
  transfers between devices with their start and end apart: 9, of which 4 were waited for; matrix products, arithmetic and copies ran while one was open for 3% of the time, Pallas kernels for 7%

profile of v4, /device:TPU:134, one launch (start us, length us, event | category | flops | bytes accessed | tf_op | source)
XLA Modules:
  0.0 125.7 jit_solution(6490163406891587365)
XLA Ops:
  0.6 0.0 copy-start.5
  0.6 2.7 %collective-permute-start = (f32[512,256]{1,0:T(8,128)}, f32[512,256]{1,0:T(8,128)S(1)}, u32[]{:S(2)}, u32[]{:S(2)}) collective-permute-start(f32[512,256]{1,0:T(8,128)} %refs_0_.5), channel_id=1, source_target_pairs={{0,3},{1,0},{2,1},{3,2},{4,7},{5,4},{6,5},{7,6},{8,11},{9,8},{10,9... | collective-permute-start | bytes 1572872 | tf_op jit(solution)/shard_map/ppermute | solution.py:31
  3.4 4.3 %collective-permute-start.2 = (f32[512,256]{1,0:T(8,128)}, f32[512,256]{1,0:T(8,128)}, u32[]{:S(2)}, u32[]{:S(2)}) collective-permute-start(f32[512,256]{1,0:T(8,128)} %refs_0_.5), channel_id=1, source_target_pairs={{0,1},{1,2},{2,3},{3,0},{4,5},{5,6},{6,7},{7,4},{8,9},{9,10},{10,1... | collective-permute-start | bytes 1572872 | tf_op jit(solution)/shard_map/ppermute | solution.py:31
  7.7 1.2 broadcast_multiply_fusion
  8.9 0.9 constant_dynamic-slice_fusion
  9.8 9.8 %collective-permute-start.5 = (f32[512,128]{1,0:T(8,128)}, f32[512,128]{1,0:T(8,128)}, u32[]{:S(2)}, u32[]{:S(2)}) collective-permute-start(f32[512,128]{1,0:T(8,128)} %get-tuple-element.22), channel_id=1, source_target_pairs={{0,12},{1,13},{2,14},{3,15},{4,8},{5,9},{6,10},{7,11},{8,4},{9,5},... | collective-permute-start | bytes 786440 | tf_op jit(solution)/shard_map/ppermute | solution.py:31
  19.6 0.0 collective-permute-done.refs_1_
  19.6 0.0 copy-start
  19.6 0.8 copy-done
  20.4 0.0 copy-done.5
  20.4 0.1 copy.13.weight_ref
  20.6 2.1 %collective-permute-start.1 = (f32[512,256]{1,0:T(8,128)}, f32[512,256]{1,0:T(8,128)}, u32[]{:S(2)}, u32[]{:S(2)}) collective-permute-start(f32[512,256]{1,0:T(8,128)} %refs_0_.5), channel_id=1, source_target_pairs={{0,2},{1,3},{2,0},{3,1},{4,6},{5,7},{6,4},{7,5},{8,10},{9,11},{10,... | collective-permute-start | bytes 1572872 | tf_op jit(solution)/shard_map/ppermute | solution.py:31
  22.7 0.0 copy-start.1
  22.7 0.0 copy-start.6
  22.7 0.0 copy-start.7
  22.7 0.0 copy-start.2
  22.7 1.2 shard_map.50.columns_ref
  24.0 0.0 copy-done.1
  24.0 0.1 slice_reduce_fusion
  24.1 0.0 copy-done.6
  24.1 0.0 copy-done.7
  24.1 0.0 copy-done.2
  24.2 0.7 select_maximum_fusion
  24.9 8.9 %collective-permute-start.4 = (f32[520,128]{1,0:T(8,128)}, f32[520,128]{1,0:T(8,128)}, u32[]{:S(2)}, u32[]{:S(2)}) collective-permute-start(f32[520,128]{1,0:T(8,128)} %select_maximum_fusion), channel_id=1, source_target_pairs={{0,4},{1,5},{2,6},{3,7},{4,0},{5,1},{6,2},{7,3},{8,12},{9,13},{10,... | collective-permute-start | bytes 798728 | tf_op jit(solution)/shard_map/ppermute | solution.py:31
  33.8 0.0 collective-permute-done.2.refs_3_
  33.8 5.0 %collective-permute-done.1.refs_2_ = f32[512,256]{1,0:T(8,128)} collective-permute-done((f32[512,256]{1,0:T(8,128)}, f32[512,256]{1,0:T(8,128)}, u32[]{:S(2)}, u32[]{:S(2)}) %collective-permute-start.1) | collective-permute-done | bytes 524320 | tf_op jit(solution)/shard_map/ppermute | solution.py:31
  38.8 3.5 %shard_map.51 = f32[8,128,256]{2,1,0:T(8,128)} custom-call(f32[512,256]{1,0:T(8,128)S(1)} %shard_map.50.columns_ref, f32[512,256]{1,0:T(8,128)} %refs_0_.5, f32[512,256]{1,0:T(8,128)S(1)} %copy-done.1, f32[512,256]{1,0:T(8,128)} %collective-permute-done.1.refs_2_, f32[512,256]{1,0:T(8,128)} %collective-permute-done.2.refs_3_), custom_call_target="tpu_custom_call" | custom-call | flops 1073741824 | bytes 8388608 | tf_op jit(solution)/shard_map/pallas_call | solution.py:44
  42.3 4.5 %all-to-all-start = ((f32[8,128,256]{2,1,0:T(8,128)}), f32[8,128,256]{2,1,0:T(8,128)}, u32[]{:S(2)}, u32[]{:S(2)}) async-start(f32[8,128,256]{2,1,0:T(8,128)} %shard_map.51), calls=%async_computation | async-start | bytes 2097152 | tf_op jit(solution)/shard_map/all_to_all | solution.py:194
  46.8 2.8 %shard_map.52.blocks_ref = f32[4,512,256]{2,1,0:T(8,128)} custom-call(f32[512,256]{1,0:T(8,128)} %refs_0_.5, f32[512,256]{1,0:T(8,128)S(1)} %copy-done.1, f32[512,256]{1,0:T(8,128)} %collective-permute-done.1.refs_2_, f32[512,256]{1,0:T(8,128)} %collective-permute-done.2.refs_3_), custom_call_target="tpu_custom_call" | custom-call | flops 274877906944 | bytes 8388608 | tf_op jit(solution)/shard_map/pallas_call | solution.py:44
  49.7 2.4 %collective-permute-start.3 = (f32[4,512,256]{2,1,0:T(8,128)}, f32[4,512,256]{2,1,0:T(8,128)}, u32[]{:S(2)}, u32[]{:S(2)}) collective-permute-start(f32[4,512,256]{2,1,0:T(8,128)} %shard_map.52.blocks_ref), channel_id=1, source_target_pairs={{0,8},{1,9},{2,10},{3,11},{4,12},{5,13},{6,14},{7,15},{8,0},{9,1},... | collective-permute-start | bytes 6291464 | tf_op jit(solution)/shard_map/ppermute | solution.py:31
  52.1 1.8 %shard_map.53.edges_ref = f32[8,8,128]{2,1,0:T(8,128)S(1)} custom-call(f32[8,512]{1,0:T(8,128)S(1)} %select_maximum_fusion.2.after_ref, f32[512,256]{1,0:T(8,128)} %refs_0_.5, f32[512,256]{1,0:T(8,128)S(1)} %copy-done.1, f32[512,256]{1,0:T(8,128)} %collective-permute-done.1.refs_2_, f32[512,256]{1,0:T(8,128)} %collective-permute-done.2.refs_3_), custom_call_target="tpu_custom_call" | custom-call | flops 274877906944 | bytes 8388608 | tf_op jit(solution)/shard_map/pallas_call | solution.py:44
  53.9 9.0 %all-to-all-done = f32[8,128,256]{2,1,0:T(8,128)} async-done(((f32[8,128,256]{2,1,0:T(8,128)}), f32[8,128,256]{2,1,0:T(8,128)}, u32[]{:S(2)}, u32[]{:S(2)}) %all-to-all-start) | async-done | bytes 1048608 | tf_op jit(solution)/shard_map/all_to_all | solution.py:194
  62.9 1.3 %reduce_sum.36 = f32[128,256]{1,0:T(8,128)S(1)} reduce(f32[8,128,256]{2,1,0:T(8,128)} %all-to-all-done, f32[]{:T(128)} %constant.30.clone.1), dimensions={0}, to_apply=%region_0.1 | reduce | flops 229376 | bytes 1179652 | tf_op jit(solution)/shard_map/reduce_sum | solution.py:195
  64.2 0.0 collective-permute-done.5.other_ref
  64.2 0.0 collective-permute-done.4.same_ref
  64.2 0.0 collective-permute-done.3.others_ref
  64.2 0.7 slice.30
  64.9 4.6 %shard_map.54 = f32[8,136,128]{2,1,0:T(8,128)} custom-call(f32[8,512]{1,0:T(8,128)S(1)} %pad.18.far_ref, f32[8,8,128]{2,1,0:T(8,128)S(1)} %shard_map.53.edges_ref, f32[520,128]{1,0:T(8,128)} %collective-permute-done.4.same_ref, f32[512,128]{1,0:T(8,128)} %collective-permute-done.5.other_ref, f32[4,512,256]{2,1,0:T(8,128)} %shard_map.52.blocks_ref, ...), custom_call_target="tpu_custom_call" | custom-call | flops 1073741824 | bytes 8388608 | tf_op jit(solution)/shard_map/pallas_call | solution.py:44
  69.5 3.5 %all-to-all-start.1 = ((f32[8,136,128]{2,1,0:T(8,128)}), f32[8,136,128]{2,1,0:T(8,128)S(1)}, u32[]{:S(2)}, u32[]{:S(2)}) async-start(f32[8,136,128]{2,1,0:T(8,128)} %shard_map.54), calls=%async_computation.1 | async-start | bytes 1114112 | tf_op jit(solution)/shard_map/all_to_all | solution.py:217
  73.0 10.6 %all-to-all-done.1 = f32[8,136,128]{2,1,0:T(8,128)S(1)} async-done(((f32[8,136,128]{2,1,0:T(8,128)}), f32[8,136,128]{2,1,0:T(8,128)S(1)}, u32[]{:S(2)}, u32[]{:S(2)}) %all-to-all-start.1) | async-done | bytes 557088 | tf_op jit(solution)/shard_map/all_to_all | solution.py:217
  83.7 0.1 stack.21
  83.8 0.1 stack.22
  83.9 0.1 fusion.2
  84.1 28.9 %all_to_all.15 = f32[8,72,128]{2,1,0:T(8,128)S(1)} all-to-all(f32[8,72,128]{2,1,0:T(8,128)S(1)} %maximum_select_fusion), channel_id=1, replica_groups=mesh['zl'=8,'y'=4,'c'=2,'zh'=2,'x'=4] {'zl'}, dimensions={0} | all-to-all | bytes 589824 | tf_op jit(solution)/shard_map/all_to_all | solution.py:235
  113.1 5.8 %collective-permute-start.6 = (f32[72,128]{1,0:T(8,128)S(1)}, f32[72,128]{1,0:T(8,128)S(1)}, u32[]{:S(2)}, u32[]{:S(2)}) collective-permute-start(f32[72,128]{1,0:T(8,128)S(1)} %reduce_sum.39.mine_ref), channel_id=1, source_target_pairs={{4,256},{5,257},{6,258},{7,259},{12,264},{13,265},{14,266},{15,267... | collective-permute-start | bytes 110600 | tf_op jit(solution)/shard_map/ppermute | solution.py:31
  118.9 4.6 %collective-permute-done.6.sent_ref = f32[72,128]{1,0:T(8,128)S(1)} collective-permute-done((f32[72,128]{1,0:T(8,128)S(1)}, f32[72,128]{1,0:T(8,128)S(1)}, u32[]{:S(2)}, u32[]{:S(2)}) %collective-permute-start.6) | collective-permute-done | bytes 36896 | tf_op jit(solution)/shard_map/ppermute | solution.py:31
  123.6 0.6 copy-done.4
  124.2 1.5 %shard_map.55 = (f32[32,256]{1,0:T(8,128)}, f32[32,256]{1,0:T(8,128)}) custom-call(s32[1]{0:T(128)} %bitcast.moved_ref, f32[72,128]{1,0:T(8,128)} %copy-done.3, f32[72,128]{1,0:T(8,128)} %copy-done.4), custom_call_target="tpu_custom_call" | custom-call | tf_op jit(solution)/shard_map/pallas_call | solution.py:145
  (17 shorter events, 0.2 us)
Async XLA Ops:
  0.6 19.8 %copy-start.5 = (f32[512]{0:T(512)S(1)}, f32[512]{0:T(512)}, u32[]{:S(2)}) copy-start(f32[512]{0:T(512)} %param.5) | copy-start | bytes 6148
  0.6 19.0 %collective-permute-start = (f32[512,256]{1,0:T(8,128)}, f32[512,256]{1,0:T(8,128)S(1)}, u32[]{:S(2)}, u32[]{:S(2)}) collective-permute-start(f32[512,256]{1,0:T(8,128)} %refs_0_.5), channel_id=1, source_target_pairs={{0,3},{1,0},{2,1},{3,2},{4,7},{5,4},{6,5},{7,6},{8,11},{9,8},{10,9... | collective-permute-start | bytes 1572872 | tf_op jit(solution)/shard_map/ppermute | solution.py:31
  3.4 30.4 %collective-permute-start.2 = (f32[512,256]{1,0:T(8,128)}, f32[512,256]{1,0:T(8,128)}, u32[]{:S(2)}, u32[]{:S(2)}) collective-permute-start(f32[512,256]{1,0:T(8,128)} %refs_0_.5), channel_id=1, source_target_pairs={{0,1},{1,2},{2,3},{3,0},{4,5},{5,6},{6,7},{7,4},{8,9},{9,10},{10,1... | collective-permute-start | bytes 1572872 | tf_op jit(solution)/shard_map/ppermute | solution.py:31
  9.8 54.4 %collective-permute-start.5 = (f32[512,128]{1,0:T(8,128)}, f32[512,128]{1,0:T(8,128)}, u32[]{:S(2)}, u32[]{:S(2)}) collective-permute-start(f32[512,128]{1,0:T(8,128)} %get-tuple-element.22), channel_id=1, source_target_pairs={{0,12},{1,13},{2,14},{3,15},{4,8},{5,9},{6,10},{7,11},{8,4},{9,5},... | collective-permute-start | bytes 786440 | tf_op jit(solution)/shard_map/ppermute | solution.py:31
  19.6 0.8 copy-start
  20.6 18.2 %collective-permute-start.1 = (f32[512,256]{1,0:T(8,128)}, f32[512,256]{1,0:T(8,128)}, u32[]{:S(2)}, u32[]{:S(2)}) collective-permute-start(f32[512,256]{1,0:T(8,128)} %refs_0_.5), channel_id=1, source_target_pairs={{0,2},{1,3},{2,0},{3,1},{4,6},{5,7},{6,4},{7,5},{8,10},{9,11},{10,... | collective-permute-start | bytes 1572872 | tf_op jit(solution)/shard_map/ppermute | solution.py:31
  22.7 1.3 %copy-start.1 = (f32[512,256]{1,0:T(8,128)S(1)}, f32[512,256]{1,0:T(8,128)}, u32[]{:S(2)}) copy-start(f32[512,256]{1,0:T(8,128)} %copy-done) | copy-start | bytes 1572868
  22.7 1.4 %copy-start.6 = (f32[512]{0:T(512)S(1)}, f32[512]{0:T(512)}, u32[]{:S(2)}) copy-start(f32[512]{0:T(512)} %param.5) | copy-start | bytes 6148
  22.7 1.4 %copy-start.7 = (f32[512]{0:T(512)S(1)}, f32[512]{0:T(512)}, u32[]{:S(2)}) copy-start(f32[512]{0:T(512)} %param.4) | copy-start | bytes 6148
  22.7 1.4 %copy-start.2 = (f32[512,128]{1,0:T(8,128)S(1)}, f32[512,128]{1,0:T(8,128)}, u32[]{:S(2)}) copy-start(f32[512,128]{1,0:T(8,128)} %get-tuple-element.13) | copy-start | bytes 786436
  24.9 39.4 %collective-permute-start.4 = (f32[520,128]{1,0:T(8,128)}, f32[520,128]{1,0:T(8,128)}, u32[]{:S(2)}, u32[]{:S(2)}) collective-permute-start(f32[520,128]{1,0:T(8,128)} %select_maximum_fusion), channel_id=1, source_target_pairs={{0,4},{1,5},{2,6},{3,7},{4,0},{5,1},{6,2},{7,3},{8,12},{9,13},{10,... | collective-permute-start | bytes 798728 | tf_op jit(solution)/shard_map/ppermute | solution.py:31
  42.3 20.6 %all-to-all-start = ((f32[8,128,256]{2,1,0:T(8,128)}), f32[8,128,256]{2,1,0:T(8,128)}, u32[]{:S(2)}, u32[]{:S(2)}) async-start(f32[8,128,256]{2,1,0:T(8,128)} %shard_map.51), calls=%async_computation | async-start | bytes 2097152 | tf_op jit(solution)/shard_map/all_to_all | solution.py:194
  49.7 14.6 %collective-permute-start.3 = (f32[4,512,256]{2,1,0:T(8,128)}, f32[4,512,256]{2,1,0:T(8,128)}, u32[]{:S(2)}, u32[]{:S(2)}) collective-permute-start(f32[4,512,256]{2,1,0:T(8,128)} %shard_map.52.blocks_ref), channel_id=1, source_target_pairs={{0,8},{1,9},{2,10},{3,11},{4,12},{5,13},{6,14},{7,15},{8,0},{9,1},... | collective-permute-start | bytes 6291464 | tf_op jit(solution)/shard_map/ppermute | solution.py:31
  69.5 14.2 %all-to-all-start.1 = ((f32[8,136,128]{2,1,0:T(8,128)}), f32[8,136,128]{2,1,0:T(8,128)S(1)}, u32[]{:S(2)}, u32[]{:S(2)}) async-start(f32[8,136,128]{2,1,0:T(8,128)} %shard_map.54), calls=%async_computation.1 | async-start | bytes 1114112 | tf_op jit(solution)/shard_map/all_to_all | solution.py:217
  113.1 10.5 %copy-start.3 = (f32[72,128]{1,0:T(8,128)}, f32[72,128]{1,0:T(8,128)S(1)}, u32[]{:S(2)}) copy-start(f32[72,128]{1,0:T(8,128)S(1)} %reduce_sum.39.mine_ref) | copy-start | bytes 110596
  113.1 10.5 %collective-permute-start.6 = (f32[72,128]{1,0:T(8,128)S(1)}, f32[72,128]{1,0:T(8,128)S(1)}, u32[]{:S(2)}, u32[]{:S(2)}) collective-permute-start(f32[72,128]{1,0:T(8,128)S(1)} %reduce_sum.39.mine_ref), channel_id=1, source_target_pairs={{4,256},{5,257},{6,258},{7,259},{12,264},{13,265},{14,266},{15,267... | collective-permute-start | bytes 110600 | tf_op jit(solution)/shard_map/ppermute | solution.py:31
  123.6 0.6 copy-start.4

commit v5 on v4

--- a/solution.py
+++ b/solution.py
@@ -104,23 +104,26 @@
         refs[-1][g] = rows_of(values, g)
 
 
-def second_kernel(
-    far_ref, edges_ref, same_ref, other_ref, blocks_ref, others_ref, out_ref
-):
+def second_kernel(edges_ref, same_ref, other_ref, blocks_ref, others_ref, out_ref):
     count, points, width = blocks_ref.shape
     size = other_ref.shape[1]
     r = width // (Y * C)
+    far = jnp.concatenate(
+        [same_ref[points + k : points + k + 1] for k in range(points // size)], axis=1
+    )
+    far = jnp.broadcast_to(far, (PAD, points)).T[:, :1]
     here = prepare(same_ref[:points])
     there = prepare(other_ref[...])
-    edge_high, edge_low = split(far_ref[...])
-    edge = (edge_high, jnp.concatenate([edge_high, edge_low], axis=0))
-    edges = []
+    values = []
     for k in range(count):
-        value = product(here, blocks_ref[k]) + product(there, others_ref[k])
+        block = blocks_ref[k]
+        value = product(here, block) + product(there, others_ref[k])
         out_ref[:, k * r : (k + 1) * r, :] = value.T.reshape(Y * C, r, size)
-        edges.append(product(edge, blocks_ref[k]))
+        values.append(jnp.sum(block * far, axis=0, keepdims=True))
+    line = lax.broadcasted_iota(jnp.int32, (PAD, count * r), 0)
     for g in range(Y * C):
-        out_ref[g, count * r :, :] = edges_ref[g] + rows_of(edges, g)
+        row = jnp.broadcast_to(rows_of(values, g), (PAD, count * r))
+        out_ref[g, count * r :, :] = edges_ref[g] + jnp.where(line == 2, row, 0.0)
 
 
 def finish_kernel(moved_ref, mine_ref, sent_ref, tile_ref, later_ref):
@@ -201,13 +204,10 @@
         (own, stack, others, same, other, edges)
     )
 
-    far = same[points : points + points // half].reshape(1, points)
-    far = jnp.pad(far, ((2, PAD - 3), (0, 0)))
     cross = call(
         second_kernel,
         (Y * C, X * r + PAD, half),
         1 << 30,
-        far,
         edges,
         same,
         other,

time: 126 us -> 126 us (level)
  transfers between devices with their start and end apart: 9 -> 9, of which waited for: 4 -> 4; matrix products, arithmetic and copies ran while one was open for 3% -> 4% of each run, Pallas kernels for 7% -> 8%
where the time goes in v5:
time: 126 us; the launch traced here: 125 us
  starting transfers between devices  44.1 us (35%)
  waiting for transfers between devices  29.2 us (23%)
  blocking collectives  28.9 us (23%)
  Pallas kernels  15.4 us (12%)
  other arithmetic  3.49 us (3%)
  local copies, waits for them, and re-layouts  2.76 us (2%)
    ppermute x7, starting transfers between devices, send(): return lax.ppermute(value, NAMES, routes(move))  36.1 us
    all_to_all x1, blocking collectives, shards(): total = lax.all_to_all(sides(own, cross), 'zl', 0, 0, tiled=True)  28.9 us
    pallas_call x5, Pallas kernels, call(): pl.pallas_call(kernel, out_shape=jax.ShapeDtypeStruct(out, jnp.float32),...  13.9 us
    all_to_all x1, waiting for transfers between devices, shards(): cross = lax.all_to_all(cross, ('y', 'c'), 0, 0, tiled=True)  10.6 us
    ppermute x7, waiting for transfers between devices, send(): return lax.ppermute(value, NAMES, routes(move))  9.61 us
    all_to_all x1, waiting for transfers between devices, shards(): own = lax.all_to_all(own, ('y', 'c'), 0, 0, tiled=True)  9.01 us
    all_to_all x1, starting transfers between devices, shards(): own = lax.all_to_all(own, ('y', 'c'), 0, 0, tiled=True)  4.5 us
    all_to_all x1, starting transfers between devices, shards(): cross = lax.all_to_all(cross, ('y', 'c'), 0, 0, tiled=True)  3.54 us
  transfers between devices with their start and end apart: 9, of which 4 were waited for; matrix products, arithmetic and copies ran while one was open for 4% of the time, Pallas kernels for 8%

profile of v5, /device:TPU:134, one launch (start us, length us, event | category | flops | bytes accessed | tf_op | source)
XLA Modules:
  0.0 124.9 jit_solution(9322806229301539161)
XLA Ops:
  0.6 0.0 copy-start.5
  0.6 2.7 %collective-permute-start = (f32[512,256]{1,0:T(8,128)}, f32[512,256]{1,0:T(8,128)S(1)}, u32[]{:S(2)}, u32[]{:S(2)}) collective-permute-start(f32[512,256]{1,0:T(8,128)} %refs_0_.5), channel_id=1, source_target_pairs={{0,3},{1,0},{2,1},{3,2},{4,7},{5,4},{6,5},{7,6},{8,11},{9,8},{10,9... | collective-permute-start | bytes 1572872 | tf_op jit(solution)/shard_map/ppermute | solution.py:31
  3.4 4.3 %collective-permute-start.2 = (f32[512,256]{1,0:T(8,128)}, f32[512,256]{1,0:T(8,128)}, u32[]{:S(2)}, u32[]{:S(2)}) collective-permute-start(f32[512,256]{1,0:T(8,128)} %refs_0_.5), channel_id=1, source_target_pairs={{0,1},{1,2},{2,3},{3,0},{4,5},{5,6},{6,7},{7,4},{8,9},{9,10},{10,1... | collective-permute-start | bytes 1572872 | tf_op jit(solution)/shard_map/ppermute | solution.py:31
  7.7 1.2 broadcast_multiply_fusion
  8.9 0.9 constant_dynamic-slice_fusion
  9.8 9.8 %collective-permute-start.5 = (f32[512,128]{1,0:T(8,128)}, f32[512,128]{1,0:T(8,128)}, u32[]{:S(2)}, u32[]{:S(2)}) collective-permute-start(f32[512,128]{1,0:T(8,128)} %get-tuple-element.22), channel_id=1, source_target_pairs={{0,12},{1,13},{2,14},{3,15},{4,8},{5,9},{6,10},{7,11},{8,4},{9,5},... | collective-permute-start | bytes 786440 | tf_op jit(solution)/shard_map/ppermute | solution.py:31
  19.6 0.0 collective-permute-done.refs_1_
  19.6 0.0 copy-start
  19.6 0.8 copy-done
  20.4 0.0 copy-done.5
  20.4 0.1 copy.13.weight_ref
  20.6 2.1 %collective-permute-start.1 = (f32[512,256]{1,0:T(8,128)}, f32[512,256]{1,0:T(8,128)}, u32[]{:S(2)}, u32[]{:S(2)}) collective-permute-start(f32[512,256]{1,0:T(8,128)} %refs_0_.5), channel_id=1, source_target_pairs={{0,2},{1,3},{2,0},{3,1},{4,6},{5,7},{6,4},{7,5},{8,10},{9,11},{10,... | collective-permute-start | bytes 1572872 | tf_op jit(solution)/shard_map/ppermute | solution.py:31
  22.7 0.0 copy-start.1
  22.7 0.0 copy-start.6
  22.7 0.0 copy-start.7
  22.7 0.0 copy-start.2
  22.7 1.2 shard_map.50.columns_ref
  24.0 0.0 copy-done.1
  24.0 0.1 slice_reduce_fusion
  24.1 0.0 copy-done.6
  24.1 0.0 copy-done.7
  24.1 0.0 copy-done.2
  24.2 0.7 select_maximum_fusion
  24.9 8.9 %collective-permute-start.4 = (f32[520,128]{1,0:T(8,128)}, f32[520,128]{1,0:T(8,128)}, u32[]{:S(2)}, u32[]{:S(2)}) collective-permute-start(f32[520,128]{1,0:T(8,128)} %select_maximum_fusion), channel_id=1, source_target_pairs={{0,4},{1,5},{2,6},{3,7},{4,0},{5,1},{6,2},{7,3},{8,12},{9,13},{10,... | collective-permute-start | bytes 798728 | tf_op jit(solution)/shard_map/ppermute | solution.py:31
  33.8 0.0 collective-permute-done.2.refs_3_
  33.8 5.0 %collective-permute-done.1.refs_2_ = f32[512,256]{1,0:T(8,128)} collective-permute-done((f32[512,256]{1,0:T(8,128)}, f32[512,256]{1,0:T(8,128)}, u32[]{:S(2)}, u32[]{:S(2)}) %collective-permute-start.1) | collective-permute-done | bytes 524320 | tf_op jit(solution)/shard_map/ppermute | solution.py:31
  38.8 3.5 %shard_map.51 = f32[8,128,256]{2,1,0:T(8,128)} custom-call(f32[512,256]{1,0:T(8,128)S(1)} %shard_map.50.columns_ref, f32[512,256]{1,0:T(8,128)} %refs_0_.5, f32[512,256]{1,0:T(8,128)S(1)} %copy-done.1, f32[512,256]{1,0:T(8,128)} %collective-permute-done.1.refs_2_, f32[512,256]{1,0:T(8,128)} %collective-permute-done.2.refs_3_), custom_call_target="tpu_custom_call" | custom-call | flops 1073741824 | bytes 8388608 | tf_op jit(solution)/shard_map/pallas_call | solution.py:44
  42.3 4.5 %all-to-all-start = ((f32[8,128,256]{2,1,0:T(8,128)}), f32[8,128,256]{2,1,0:T(8,128)}, u32[]{:S(2)}, u32[]{:S(2)}) async-start(f32[8,128,256]{2,1,0:T(8,128)} %shard_map.51), calls=%async_computation | async-start | bytes 2097152 | tf_op jit(solution)/shard_map/all_to_all | solution.py:197
  46.8 2.8 %shard_map.52.blocks_ref = f32[4,512,256]{2,1,0:T(8,128)} custom-call(f32[512,256]{1,0:T(8,128)} %refs_0_.5, f32[512,256]{1,0:T(8,128)S(1)} %copy-done.1, f32[512,256]{1,0:T(8,128)} %collective-permute-done.1.refs_2_, f32[512,256]{1,0:T(8,128)} %collective-permute-done.2.refs_3_), custom_call_target="tpu_custom_call" | custom-call | flops 274877906944 | bytes 8388608 | tf_op jit(solution)/shard_map/pallas_call | solution.py:44
  49.7 2.4 %collective-permute-start.3 = (f32[4,512,256]{2,1,0:T(8,128)}, f32[4,512,256]{2,1,0:T(8,128)}, u32[]{:S(2)}, u32[]{:S(2)}) collective-permute-start(f32[4,512,256]{2,1,0:T(8,128)} %shard_map.52.blocks_ref), channel_id=1, source_target_pairs={{0,8},{1,9},{2,10},{3,11},{4,12},{5,13},{6,14},{7,15},{8,0},{9,1},... | collective-permute-start | bytes 6291464 | tf_op jit(solution)/shard_map/ppermute | solution.py:31
  52.1 1.8 %shard_map.53.edges_ref = f32[8,8,128]{2,1,0:T(8,128)S(1)} custom-call(f32[8,512]{1,0:T(8,128)S(1)} %select_maximum_fusion.2.after_ref, f32[512,256]{1,0:T(8,128)} %refs_0_.5, f32[512,256]{1,0:T(8,128)S(1)} %copy-done.1, f32[512,256]{1,0:T(8,128)} %collective-permute-done.1.refs_2_, f32[512,256]{1,0:T(8,128)} %collective-permute-done.2.refs_3_), custom_call_target="tpu_custom_call" | custom-call | flops 274877906944 | bytes 8388608 | tf_op jit(solution)/shard_map/pallas_call | solution.py:44
  53.9 9.0 %all-to-all-done = f32[8,128,256]{2,1,0:T(8,128)} async-done(((f32[8,128,256]{2,1,0:T(8,128)}), f32[8,128,256]{2,1,0:T(8,128)}, u32[]{:S(2)}, u32[]{:S(2)}) %all-to-all-start) | async-done | bytes 1048608 | tf_op jit(solution)/shard_map/all_to_all | solution.py:197
  62.9 1.3 %reduce_sum.36 = f32[128,256]{1,0:T(8,128)S(1)} reduce(f32[8,128,256]{2,1,0:T(8,128)} %all-to-all-done, f32[]{:T(128)} %constant.30.clone.1), dimensions={0}, to_apply=%region_0.1 | reduce | flops 229376 | bytes 1179652 | tf_op jit(solution)/shard_map/reduce_sum | solution.py:198
  64.2 0.0 collective-permute-done.5.other_ref
  64.2 0.0 collective-permute-done.4.same_ref
  64.2 0.0 collective-permute-done.3.others_ref
  64.2 4.5 %shard_map.54 = f32[8,136,128]{2,1,0:T(8,128)} custom-call(f32[8,8,128]{2,1,0:T(8,128)S(1)} %shard_map.53.edges_ref, f32[520,128]{1,0:T(8,128)} %collective-permute-done.4.same_ref, f32[512,128]{1,0:T(8,128)} %collective-permute-done.5.other_ref, f32[4,512,256]{2,1,0:T(8,128)} %shard_map.52.blocks_ref, f32[4,512,256]{2,1,0:T(8,128)} %collective-permute-done.3.others_ref), custom_call_target="tpu_custom_call" | custom-call | flops 1073741824 | bytes 8388608 | tf_op jit(solution)/shard_map/pallas_call | solution.py:44
  68.7 3.5 %all-to-all-start.1 = ((f32[8,136,128]{2,1,0:T(8,128)}), f32[8,136,128]{2,1,0:T(8,128)S(1)}, u32[]{:S(2)}, u32[]{:S(2)}) async-start(f32[8,136,128]{2,1,0:T(8,128)} %shard_map.54), calls=%async_computation.1 | async-start | bytes 1114112 | tf_op jit(solution)/shard_map/all_to_all | solution.py:217
  72.3 10.6 %all-to-all-done.1 = f32[8,136,128]{2,1,0:T(8,128)S(1)} async-done(((f32[8,136,128]{2,1,0:T(8,128)}), f32[8,136,128]{2,1,0:T(8,128)S(1)}, u32[]{:S(2)}, u32[]{:S(2)}) %all-to-all-start.1) | async-done | bytes 557088 | tf_op jit(solution)/shard_map/all_to_all | solution.py:217
  83.0 0.1 stack.21
  83.0 0.1 stack.22
  83.2 0.1 fusion.2
  83.3 28.9 %all_to_all.15 = f32[8,72,128]{2,1,0:T(8,128)S(1)} all-to-all(f32[8,72,128]{2,1,0:T(8,128)S(1)} %maximum_select_fusion), channel_id=1, replica_groups=mesh['zl'=8,'y'=4,'c'=2,'zh'=2,'x'=4] {'zl'}, dimensions={0} | all-to-all | bytes 589824 | tf_op jit(solution)/shard_map/all_to_all | solution.py:235
  112.3 0.0 copy-start.3
  112.3 5.8 %collective-permute-start.6 = (f32[72,128]{1,0:T(8,128)S(1)}, f32[72,128]{1,0:T(8,128)S(1)}, u32[]{:S(2)}, u32[]{:S(2)}) collective-permute-start(f32[72,128]{1,0:T(8,128)S(1)} %reduce_sum.39.mine_ref), channel_id=1, source_target_pairs={{4,256},{5,257},{6,258},{7,259},{12,264},{13,265},{14,266},{15,267... | collective-permute-start | bytes 110600 | tf_op jit(solution)/shard_map/ppermute | solution.py:31
  118.2 4.6 %collective-permute-done.6.sent_ref = f32[72,128]{1,0:T(8,128)S(1)} collective-permute-done((f32[72,128]{1,0:T(8,128)S(1)}, f32[72,128]{1,0:T(8,128)S(1)}, u32[]{:S(2)}, u32[]{:S(2)}) %collective-permute-start.6) | collective-permute-done | bytes 36896 | tf_op jit(solution)/shard_map/ppermute | solution.py:31
  122.8 0.6 copy-done.4
  123.4 1.5 %shard_map.55 = (f32[32,256]{1,0:T(8,128)}, f32[32,256]{1,0:T(8,128)}) custom-call(s32[1]{0:T(128)} %bitcast.moved_ref, f32[72,128]{1,0:T(8,128)} %copy-done.3, f32[72,128]{1,0:T(8,128)} %copy-done.4), custom_call_target="tpu_custom_call" | custom-call | tf_op jit(solution)/shard_map/pallas_call | solution.py:148
  (15 shorter events, 0.2 us)
Async XLA Ops:
  0.6 19.8 %copy-start.5 = (f32[512]{0:T(512)S(1)}, f32[512]{0:T(512)}, u32[]{:S(2)}) copy-start(f32[512]{0:T(512)} %param.5) | copy-start | bytes 6148
  0.6 19.0 %collective-permute-start = (f32[512,256]{1,0:T(8,128)}, f32[512,256]{1,0:T(8,128)S(1)}, u32[]{:S(2)}, u32[]{:S(2)}) collective-permute-start(f32[512,256]{1,0:T(8,128)} %refs_0_.5), channel_id=1, source_target_pairs={{0,3},{1,0},{2,1},{3,2},{4,7},{5,4},{6,5},{7,6},{8,11},{9,8},{10,9... | collective-permute-start | bytes 1572872 | tf_op jit(solution)/shard_map/ppermute | solution.py:31
  3.4 30.4 %collective-permute-start.2 = (f32[512,256]{1,0:T(8,128)}, f32[512,256]{1,0:T(8,128)}, u32[]{:S(2)}, u32[]{:S(2)}) collective-permute-start(f32[512,256]{1,0:T(8,128)} %refs_0_.5), channel_id=1, source_target_pairs={{0,1},{1,2},{2,3},{3,0},{4,5},{5,6},{6,7},{7,4},{8,9},{9,10},{10,1... | collective-permute-start | bytes 1572872 | tf_op jit(solution)/shard_map/ppermute | solution.py:31
  9.8 54.4 %collective-permute-start.5 = (f32[512,128]{1,0:T(8,128)}, f32[512,128]{1,0:T(8,128)}, u32[]{:S(2)}, u32[]{:S(2)}) collective-permute-start(f32[512,128]{1,0:T(8,128)} %get-tuple-element.22), channel_id=1, source_target_pairs={{0,12},{1,13},{2,14},{3,15},{4,8},{5,9},{6,10},{7,11},{8,4},{9,5},... | collective-permute-start | bytes 786440 | tf_op jit(solution)/shard_map/ppermute | solution.py:31
  19.6 0.8 copy-start
  20.6 18.2 %collective-permute-start.1 = (f32[512,256]{1,0:T(8,128)}, f32[512,256]{1,0:T(8,128)}, u32[]{:S(2)}, u32[]{:S(2)}) collective-permute-start(f32[512,256]{1,0:T(8,128)} %refs_0_.5), channel_id=1, source_target_pairs={{0,2},{1,3},{2,0},{3,1},{4,6},{5,7},{6,4},{7,5},{8,10},{9,11},{10,... | collective-permute-start | bytes 1572872 | tf_op jit(solution)/shard_map/ppermute | solution.py:31
  22.7 1.3 %copy-start.1 = (f32[512,256]{1,0:T(8,128)S(1)}, f32[512,256]{1,0:T(8,128)}, u32[]{:S(2)}) copy-start(f32[512,256]{1,0:T(8,128)} %copy-done) | copy-start | bytes 1572868
  22.7 1.4 %copy-start.6 = (f32[512]{0:T(512)S(1)}, f32[512]{0:T(512)}, u32[]{:S(2)}) copy-start(f32[512]{0:T(512)} %param.5) | copy-start | bytes 6148
  22.7 1.4 %copy-start.7 = (f32[512]{0:T(512)S(1)}, f32[512]{0:T(512)}, u32[]{:S(2)}) copy-start(f32[512]{0:T(512)} %param.4) | copy-start | bytes 6148
  22.7 1.4 %copy-start.2 = (f32[512,128]{1,0:T(8,128)S(1)}, f32[512,128]{1,0:T(8,128)}, u32[]{:S(2)}) copy-start(f32[512,128]{1,0:T(8,128)} %get-tuple-element.13) | copy-start | bytes 786436
  24.9 39.4 %collective-permute-start.4 = (f32[520,128]{1,0:T(8,128)}, f32[520,128]{1,0:T(8,128)}, u32[]{:S(2)}, u32[]{:S(2)}) collective-permute-start(f32[520,128]{1,0:T(8,128)} %select_maximum_fusion), channel_id=1, source_target_pairs={{0,4},{1,5},{2,6},{3,7},{4,0},{5,1},{6,2},{7,3},{8,12},{9,13},{10,... | collective-permute-start | bytes 798728 | tf_op jit(solution)/shard_map/ppermute | solution.py:31
  42.3 20.6 %all-to-all-start = ((f32[8,128,256]{2,1,0:T(8,128)}), f32[8,128,256]{2,1,0:T(8,128)}, u32[]{:S(2)}, u32[]{:S(2)}) async-start(f32[8,128,256]{2,1,0:T(8,128)} %shard_map.51), calls=%async_computation | async-start | bytes 2097152 | tf_op jit(solution)/shard_map/all_to_all | solution.py:197
  49.7 14.6 %collective-permute-start.3 = (f32[4,512,256]{2,1,0:T(8,128)}, f32[4,512,256]{2,1,0:T(8,128)}, u32[]{:S(2)}, u32[]{:S(2)}) collective-permute-start(f32[4,512,256]{2,1,0:T(8,128)} %shard_map.52.blocks_ref), channel_id=1, source_target_pairs={{0,8},{1,9},{2,10},{3,11},{4,12},{5,13},{6,14},{7,15},{8,0},{9,1},... | collective-permute-start | bytes 6291464 | tf_op jit(solution)/shard_map/ppermute | solution.py:31
  68.7 14.2 %all-to-all-start.1 = ((f32[8,136,128]{2,1,0:T(8,128)}), f32[8,136,128]{2,1,0:T(8,128)S(1)}, u32[]{:S(2)}, u32[]{:S(2)}) async-start(f32[8,136,128]{2,1,0:T(8,128)} %shard_map.54), calls=%async_computation.1 | async-start | bytes 1114112 | tf_op jit(solution)/shard_map/all_to_all | solution.py:217
  112.3 10.5 %copy-start.3 = (f32[72,128]{1,0:T(8,128)}, f32[72,128]{1,0:T(8,128)S(1)}, u32[]{:S(2)}) copy-start(f32[72,128]{1,0:T(8,128)S(1)} %reduce_sum.39.mine_ref) | copy-start | bytes 110596
  112.3 10.5 %collective-permute-start.6 = (f32[72,128]{1,0:T(8,128)S(1)}, f32[72,128]{1,0:T(8,128)S(1)}, u32[]{:S(2)}, u32[]{:S(2)}) collective-permute-start(f32[72,128]{1,0:T(8,128)S(1)} %reduce_sum.39.mine_ref), channel_id=1, source_target_pairs={{4,256},{5,257},{6,258},{7,259},{12,264},{13,265},{14,266},{15,267... | collective-permute-start | bytes 110600 | tf_op jit(solution)/shard_map/ppermute | solution.py:31
  122.8 0.6 copy-start.4

commit v6 on v5

--- a/solution.py
+++ b/solution.py
@@ -126,10 +126,11 @@
         out_ref[g, count * r :, :] = edges_ref[g] + jnp.where(line == 2, row, 0.0)
 
 
-def finish_kernel(moved_ref, mine_ref, sent_ref, tile_ref, later_ref):
+def finish_kernel(mine_ref, sent_ref, tile_ref, later_ref):
     r, width = tile_ref.shape
     half = width // 2
-    value = jnp.where(moved_ref[0] > 0, sent_ref[...], mine_ref[...])
+    moved = (lax.axis_index("zl") >= X) == (lax.axis_index("zh") == 0)
+    value = jnp.where(moved, sent_ref[...], mine_ref[...])
     tile = jnp.concatenate([value[:r], value[r : 2 * r]], axis=1)
     row = lax.broadcasted_iota(jnp.int32, (r, half), 0)
     lane = lax.broadcasted_iota(jnp.int32, (r, half), 1)
@@ -142,21 +143,21 @@
     )
 
 
-def finish(moved, mine, sent):
+def finish(mine, sent):
     r, width = (mine.shape[0] - PAD) // 2, 2 * mine.shape[1]
     vmem = pl.BlockSpec(memory_space=pltpu.VMEM)
     return pl.pallas_call(
         finish_kernel,
         out_shape=[jax.ShapeDtypeStruct((r, width), jnp.float32)] * 2,
-        in_specs=[pl.BlockSpec(memory_space=pltpu.SMEM), vmem, vmem],
+        in_specs=[vmem, vmem],
         out_specs=[vmem, vmem],
-    )(moved.astype(jnp.int32).reshape(1), mine, sent)
+    )(mine, sent)
 
 
 def shards(snapshots, following, mass):
     points, width = snapshots.shape
     half, r = width // 2, width // (Y * C)
-    x, zh, zl = lax.axis_index("x"), lax.axis_index("zh"), lax.axis_index("zl")
+    x, zh = lax.axis_index("x"), lax.axis_index("zh")
     core = lax.axis_index("c")
 
     def along_x(value, k):
@@ -234,8 +235,7 @@
     cross = slots(cross[0, : X * r], cross[1, : X * r], edges[1])
     total = lax.all_to_all(sides(own, cross), "zl", 0, 0, tiled=True)
     total = jnp.sum(total, axis=0)
-    moved = (zl >= X) == (zh == 0)
-    return finish(moved, total, send(total, home))
+    return finish(total, send(total, home))
 
 
 def solution(mesh):

time: 126 us -> 126 us (level)
  no operation moved by 1% of the time
where the time goes in v6:
time: 126 us; the launch traced here: 125 us
  starting transfers between devices  44.1 us (35%)
  waiting for transfers between devices  29.2 us (23%)
  blocking collectives  28.9 us (23%)
  Pallas kernels  15.4 us (12%)
  other arithmetic  3.49 us (3%)
  local copies, waits for them, and re-layouts  2.76 us (2%)
    ppermute x7, starting transfers between devices, send(): return lax.ppermute(value, NAMES, routes(move))  36.1 us
    all_to_all x1, blocking collectives, shards(): total = lax.all_to_all(sides(own, cross), 'zl', 0, 0, tiled=True)  28.9 us
    pallas_call x5, Pallas kernels, call(): pl.pallas_call(kernel, out_shape=jax.ShapeDtypeStruct(out, jnp.float32),...  13.9 us
    all_to_all x1, waiting for transfers between devices, shards(): cross = lax.all_to_all(cross, ('y', 'c'), 0, 0, tiled=True)  10.6 us
    ppermute x7, waiting for transfers between devices, send(): return lax.ppermute(value, NAMES, routes(move))  9.62 us
    all_to_all x1, waiting for transfers between devices, shards(): own = lax.all_to_all(own, ('y', 'c'), 0, 0, tiled=True)  9.01 us
    all_to_all x1, starting transfers between devices, shards(): own = lax.all_to_all(own, ('y', 'c'), 0, 0, tiled=True)  4.5 us
    all_to_all x1, starting transfers between devices, shards(): cross = lax.all_to_all(cross, ('y', 'c'), 0, 0, tiled=True)  3.54 us
  transfers between devices with their start and end apart: 9, of which 4 were waited for; matrix products, arithmetic and copies ran while one was open for 4% of the time, Pallas kernels for 8%

profile of v6, /device:TPU:134, one launch (start us, length us, event | category | flops | bytes accessed | tf_op | source)
XLA Modules:
  0.0 124.9 jit_solution(13451371767421674515)
XLA Ops:
  0.6 0.0 copy-start.5
  0.6 2.7 %collective-permute-start = (f32[512,256]{1,0:T(8,128)}, f32[512,256]{1,0:T(8,128)S(1)}, u32[]{:S(2)}, u32[]{:S(2)}) collective-permute-start(f32[512,256]{1,0:T(8,128)} %refs_0_.5), channel_id=1, source_target_pairs={{0,3},{1,0},{2,1},{3,2},{4,7},{5,4},{6,5},{7,6},{8,11},{9,8},{10,9... | collective-permute-start | bytes 1572872 | tf_op jit(solution)/shard_map/ppermute | solution.py:31
  3.4 4.3 %collective-permute-start.2 = (f32[512,256]{1,0:T(8,128)}, f32[512,256]{1,0:T(8,128)}, u32[]{:S(2)}, u32[]{:S(2)}) collective-permute-start(f32[512,256]{1,0:T(8,128)} %refs_0_.5), channel_id=1, source_target_pairs={{0,1},{1,2},{2,3},{3,0},{4,5},{5,6},{6,7},{7,4},{8,9},{9,10},{10,1... | collective-permute-start | bytes 1572872 | tf_op jit(solution)/shard_map/ppermute | solution.py:31
  7.7 1.2 broadcast_multiply_fusion
  8.9 0.9 constant_dynamic-slice_fusion
  9.8 9.8 %collective-permute-start.5 = (f32[512,128]{1,0:T(8,128)}, f32[512,128]{1,0:T(8,128)}, u32[]{:S(2)}, u32[]{:S(2)}) collective-permute-start(f32[512,128]{1,0:T(8,128)} %get-tuple-element.22), channel_id=1, source_target_pairs={{0,12},{1,13},{2,14},{3,15},{4,8},{5,9},{6,10},{7,11},{8,4},{9,5},... | collective-permute-start | bytes 786440 | tf_op jit(solution)/shard_map/ppermute | solution.py:31
  19.6 0.0 collective-permute-done.refs_1_
  19.6 0.0 copy-start
  19.6 0.8 copy-done
  20.4 0.0 copy-done.5
  20.4 0.1 copy.13.weight_ref
  20.6 2.1 %collective-permute-start.1 = (f32[512,256]{1,0:T(8,128)}, f32[512,256]{1,0:T(8,128)}, u32[]{:S(2)}, u32[]{:S(2)}) collective-permute-start(f32[512,256]{1,0:T(8,128)} %refs_0_.5), channel_id=1, source_target_pairs={{0,2},{1,3},{2,0},{3,1},{4,6},{5,7},{6,4},{7,5},{8,10},{9,11},{10,... | collective-permute-start | bytes 1572872 | tf_op jit(solution)/shard_map/ppermute | solution.py:31
  22.7 0.0 copy-start.1
  22.7 0.0 copy-start.6
  22.7 0.0 copy-start.7
  22.7 0.0 copy-start.2
  22.7 1.2 shard_map.50.columns_ref
  24.0 0.0 copy-done.1
  24.0 0.1 slice_reduce_fusion
  24.1 0.0 copy-done.6
  24.1 0.0 copy-done.7
  24.1 0.0 copy-done.2
  24.2 0.7 select_maximum_fusion
  24.9 8.9 %collective-permute-start.4 = (f32[520,128]{1,0:T(8,128)}, f32[520,128]{1,0:T(8,128)}, u32[]{:S(2)}, u32[]{:S(2)}) collective-permute-start(f32[520,128]{1,0:T(8,128)} %select_maximum_fusion), channel_id=1, source_target_pairs={{0,4},{1,5},{2,6},{3,7},{4,0},{5,1},{6,2},{7,3},{8,12},{9,13},{10,... | collective-permute-start | bytes 798728 | tf_op jit(solution)/shard_map/ppermute | solution.py:31
  33.8 0.0 collective-permute-done.2.refs_3_
  33.8 5.0 %collective-permute-done.1.refs_2_ = f32[512,256]{1,0:T(8,128)} collective-permute-done((f32[512,256]{1,0:T(8,128)}, f32[512,256]{1,0:T(8,128)}, u32[]{:S(2)}, u32[]{:S(2)}) %collective-permute-start.1) | collective-permute-done | bytes 524320 | tf_op jit(solution)/shard_map/ppermute | solution.py:31
  38.8 3.5 %shard_map.51 = f32[8,128,256]{2,1,0:T(8,128)} custom-call(f32[512,256]{1,0:T(8,128)S(1)} %shard_map.50.columns_ref, f32[512,256]{1,0:T(8,128)} %refs_0_.5, f32[512,256]{1,0:T(8,128)S(1)} %copy-done.1, f32[512,256]{1,0:T(8,128)} %collective-permute-done.1.refs_2_, f32[512,256]{1,0:T(8,128)} %collective-permute-done.2.refs_3_), custom_call_target="tpu_custom_call" | custom-call | flops 1073741824 | bytes 8388608 | tf_op jit(solution)/shard_map/pallas_call | solution.py:44
  42.3 4.5 %all-to-all-start = ((f32[8,128,256]{2,1,0:T(8,128)}), f32[8,128,256]{2,1,0:T(8,128)}, u32[]{:S(2)}, u32[]{:S(2)}) async-start(f32[8,128,256]{2,1,0:T(8,128)} %shard_map.51), calls=%async_computation | async-start | bytes 2097152 | tf_op jit(solution)/shard_map/all_to_all | solution.py:198
  46.8 2.8 %shard_map.52.blocks_ref = f32[4,512,256]{2,1,0:T(8,128)} custom-call(f32[512,256]{1,0:T(8,128)} %refs_0_.5, f32[512,256]{1,0:T(8,128)S(1)} %copy-done.1, f32[512,256]{1,0:T(8,128)} %collective-permute-done.1.refs_2_, f32[512,256]{1,0:T(8,128)} %collective-permute-done.2.refs_3_), custom_call_target="tpu_custom_call" | custom-call | flops 274877906944 | bytes 8388608 | tf_op jit(solution)/shard_map/pallas_call | solution.py:44
  49.7 2.4 %collective-permute-start.3 = (f32[4,512,256]{2,1,0:T(8,128)}, f32[4,512,256]{2,1,0:T(8,128)}, u32[]{:S(2)}, u32[]{:S(2)}) collective-permute-start(f32[4,512,256]{2,1,0:T(8,128)} %shard_map.52.blocks_ref), channel_id=1, source_target_pairs={{0,8},{1,9},{2,10},{3,11},{4,12},{5,13},{6,14},{7,15},{8,0},{9,1},... | collective-permute-start | bytes 6291464 | tf_op jit(solution)/shard_map/ppermute | solution.py:31
  52.1 1.8 %shard_map.53.edges_ref = f32[8,8,128]{2,1,0:T(8,128)S(1)} custom-call(f32[8,512]{1,0:T(8,128)S(1)} %select_maximum_fusion.2.after_ref, f32[512,256]{1,0:T(8,128)} %refs_0_.5, f32[512,256]{1,0:T(8,128)S(1)} %copy-done.1, f32[512,256]{1,0:T(8,128)} %collective-permute-done.1.refs_2_, f32[512,256]{1,0:T(8,128)} %collective-permute-done.2.refs_3_), custom_call_target="tpu_custom_call" | custom-call | flops 274877906944 | bytes 8388608 | tf_op jit(solution)/shard_map/pallas_call | solution.py:44
  53.9 9.0 %all-to-all-done = f32[8,128,256]{2,1,0:T(8,128)} async-done(((f32[8,128,256]{2,1,0:T(8,128)}), f32[8,128,256]{2,1,0:T(8,128)}, u32[]{:S(2)}, u32[]{:S(2)}) %all-to-all-start) | async-done | bytes 1048608 | tf_op jit(solution)/shard_map/all_to_all | solution.py:198
  62.9 1.3 %reduce_sum.36 = f32[128,256]{1,0:T(8,128)S(1)} reduce(f32[8,128,256]{2,1,0:T(8,128)} %all-to-all-done, f32[]{:T(128)} %constant.24.clone.1), dimensions={0}, to_apply=%region_0.1 | reduce | flops 229376 | bytes 1179652 | tf_op jit(solution)/shard_map/reduce_sum | solution.py:199
  64.2 0.0 collective-permute-done.5.other_ref
  64.2 0.0 collective-permute-done.4.same_ref
  64.2 0.0 collective-permute-done.3.others_ref
  64.2 4.5 %shard_map.54 = f32[8,136,128]{2,1,0:T(8,128)} custom-call(f32[8,8,128]{2,1,0:T(8,128)S(1)} %shard_map.53.edges_ref, f32[520,128]{1,0:T(8,128)} %collective-permute-done.4.same_ref, f32[512,128]{1,0:T(8,128)} %collective-permute-done.5.other_ref, f32[4,512,256]{2,1,0:T(8,128)} %shard_map.52.blocks_ref, f32[4,512,256]{2,1,0:T(8,128)} %collective-permute-done.3.others_ref), custom_call_target="tpu_custom_call" | custom-call | flops 1073741824 | bytes 8388608 | tf_op jit(solution)/shard_map/pallas_call | solution.py:44
  68.7 3.5 %all-to-all-start.1 = ((f32[8,136,128]{2,1,0:T(8,128)}), f32[8,136,128]{2,1,0:T(8,128)S(1)}, u32[]{:S(2)}, u32[]{:S(2)}) async-start(f32[8,136,128]{2,1,0:T(8,128)} %shard_map.54), calls=%async_computation.1 | async-start | bytes 1114112 | tf_op jit(solution)/shard_map/all_to_all | solution.py:218
  72.3 10.6 %all-to-all-done.1 = f32[8,136,128]{2,1,0:T(8,128)S(1)} async-done(((f32[8,136,128]{2,1,0:T(8,128)}), f32[8,136,128]{2,1,0:T(8,128)S(1)}, u32[]{:S(2)}, u32[]{:S(2)}) %all-to-all-start.1) | async-done | bytes 557088 | tf_op jit(solution)/shard_map/all_to_all | solution.py:218
  83.0 0.1 stack.21
  83.0 0.1 stack.22
  83.2 0.1 fusion.2
  83.3 28.9 %all_to_all.15 = f32[8,72,128]{2,1,0:T(8,128)S(1)} all-to-all(f32[8,72,128]{2,1,0:T(8,128)S(1)} %maximum_select_fusion), channel_id=1, replica_groups=mesh['zl'=8,'y'=4,'c'=2,'zh'=2,'x'=4] {'zl'}, dimensions={0} | all-to-all | bytes 589824 | tf_op jit(solution)/shard_map/all_to_all | solution.py:236
  112.3 0.0 copy-start.3
  112.3 5.8 %collective-permute-start.6 = (f32[72,128]{1,0:T(8,128)S(1)}, f32[72,128]{1,0:T(8,128)S(1)}, u32[]{:S(2)}, u32[]{:S(2)}) collective-permute-start(f32[72,128]{1,0:T(8,128)S(1)} %reduce_sum.39.mine_ref), channel_id=1, source_target_pairs={{4,256},{5,257},{6,258},{7,259},{12,264},{13,265},{14,266},{15,267... | collective-permute-start | bytes 110600 | tf_op jit(solution)/shard_map/ppermute | solution.py:31
  118.2 4.6 %collective-permute-done.6.sent_ref = f32[72,128]{1,0:T(8,128)S(1)} collective-permute-done((f32[72,128]{1,0:T(8,128)S(1)}, f32[72,128]{1,0:T(8,128)S(1)}, u32[]{:S(2)}, u32[]{:S(2)}) %collective-permute-start.6) | collective-permute-done | bytes 36896 | tf_op jit(solution)/shard_map/ppermute | solution.py:31
  122.8 0.6 copy-done.4
  123.4 1.5 %shard_map.55 = (f32[32,256]{1,0:T(8,128)}, f32[32,256]{1,0:T(8,128)}) custom-call(f32[72,128]{1,0:T(8,128)} %copy-done.3, f32[72,128]{1,0:T(8,128)} %copy-done.4), custom_call_target="tpu_custom_call" | custom-call | tf_op jit(solution)/shard_map/pallas_call | solution.py:149
  (15 shorter events, 0.2 us)
Async XLA Ops:
  0.6 19.8 %copy-start.5 = (f32[512]{0:T(512)S(1)}, f32[512]{0:T(512)}, u32[]{:S(2)}) copy-start(f32[512]{0:T(512)} %param.5) | copy-start | bytes 6148
  0.6 19.0 %collective-permute-start = (f32[512,256]{1,0:T(8,128)}, f32[512,256]{1,0:T(8,128)S(1)}, u32[]{:S(2)}, u32[]{:S(2)}) collective-permute-start(f32[512,256]{1,0:T(8,128)} %refs_0_.5), channel_id=1, source_target_pairs={{0,3},{1,0},{2,1},{3,2},{4,7},{5,4},{6,5},{7,6},{8,11},{9,8},{10,9... | collective-permute-start | bytes 1572872 | tf_op jit(solution)/shard_map/ppermute | solution.py:31
  3.4 30.4 %collective-permute-start.2 = (f32[512,256]{1,0:T(8,128)}, f32[512,256]{1,0:T(8,128)}, u32[]{:S(2)}, u32[]{:S(2)}) collective-permute-start(f32[512,256]{1,0:T(8,128)} %refs_0_.5), channel_id=1, source_target_pairs={{0,1},{1,2},{2,3},{3,0},{4,5},{5,6},{6,7},{7,4},{8,9},{9,10},{10,1... | collective-permute-start | bytes 1572872 | tf_op jit(solution)/shard_map/ppermute | solution.py:31
  9.8 54.4 %collective-permute-start.5 = (f32[512,128]{1,0:T(8,128)}, f32[512,128]{1,0:T(8,128)}, u32[]{:S(2)}, u32[]{:S(2)}) collective-permute-start(f32[512,128]{1,0:T(8,128)} %get-tuple-element.22), channel_id=1, source_target_pairs={{0,12},{1,13},{2,14},{3,15},{4,8},{5,9},{6,10},{7,11},{8,4},{9,5},... | collective-permute-start | bytes 786440 | tf_op jit(solution)/shard_map/ppermute | solution.py:31
  19.6 0.8 copy-start
  20.6 18.2 %collective-permute-start.1 = (f32[512,256]{1,0:T(8,128)}, f32[512,256]{1,0:T(8,128)}, u32[]{:S(2)}, u32[]{:S(2)}) collective-permute-start(f32[512,256]{1,0:T(8,128)} %refs_0_.5), channel_id=1, source_target_pairs={{0,2},{1,3},{2,0},{3,1},{4,6},{5,7},{6,4},{7,5},{8,10},{9,11},{10,... | collective-permute-start | bytes 1572872 | tf_op jit(solution)/shard_map/ppermute | solution.py:31
  22.7 1.3 %copy-start.1 = (f32[512,256]{1,0:T(8,128)S(1)}, f32[512,256]{1,0:T(8,128)}, u32[]{:S(2)}) copy-start(f32[512,256]{1,0:T(8,128)} %copy-done) | copy-start | bytes 1572868
  22.7 1.4 %copy-start.6 = (f32[512]{0:T(512)S(1)}, f32[512]{0:T(512)}, u32[]{:S(2)}) copy-start(f32[512]{0:T(512)} %param.5) | copy-start | bytes 6148
  22.7 1.4 %copy-start.7 = (f32[512]{0:T(512)S(1)}, f32[512]{0:T(512)}, u32[]{:S(2)}) copy-start(f32[512]{0:T(512)} %param.4) | copy-start | bytes 6148
  22.7 1.4 %copy-start.2 = (f32[512,128]{1,0:T(8,128)S(1)}, f32[512,128]{1,0:T(8,128)}, u32[]{:S(2)}) copy-start(f32[512,128]{1,0:T(8,128)} %get-tuple-element.13) | copy-start | bytes 786436
  24.9 39.4 %collective-permute-start.4 = (f32[520,128]{1,0:T(8,128)}, f32[520,128]{1,0:T(8,128)}, u32[]{:S(2)}, u32[]{:S(2)}) collective-permute-start(f32[520,128]{1,0:T(8,128)} %select_maximum_fusion), channel_id=1, source_target_pairs={{0,4},{1,5},{2,6},{3,7},{4,0},{5,1},{6,2},{7,3},{8,12},{9,13},{10,... | collective-permute-start | bytes 798728 | tf_op jit(solution)/shard_map/ppermute | solution.py:31
  42.3 20.6 %all-to-all-start = ((f32[8,128,256]{2,1,0:T(8,128)}), f32[8,128,256]{2,1,0:T(8,128)}, u32[]{:S(2)}, u32[]{:S(2)}) async-start(f32[8,128,256]{2,1,0:T(8,128)} %shard_map.51), calls=%async_computation | async-start | bytes 2097152 | tf_op jit(solution)/shard_map/all_to_all | solution.py:198
  49.7 14.6 %collective-permute-start.3 = (f32[4,512,256]{2,1,0:T(8,128)}, f32[4,512,256]{2,1,0:T(8,128)}, u32[]{:S(2)}, u32[]{:S(2)}) collective-permute-start(f32[4,512,256]{2,1,0:T(8,128)} %shard_map.52.blocks_ref), channel_id=1, source_target_pairs={{0,8},{1,9},{2,10},{3,11},{4,12},{5,13},{6,14},{7,15},{8,0},{9,1},... | collective-permute-start | bytes 6291464 | tf_op jit(solution)/shard_map/ppermute | solution.py:31
  68.7 14.2 %all-to-all-start.1 = ((f32[8,136,128]{2,1,0:T(8,128)}), f32[8,136,128]{2,1,0:T(8,128)S(1)}, u32[]{:S(2)}, u32[]{:S(2)}) async-start(f32[8,136,128]{2,1,0:T(8,128)} %shard_map.54), calls=%async_computation.1 | async-start | bytes 1114112 | tf_op jit(solution)/shard_map/all_to_all | solution.py:218
  112.3 10.5 %copy-start.3 = (f32[72,128]{1,0:T(8,128)}, f32[72,128]{1,0:T(8,128)S(1)}, u32[]{:S(2)}) copy-start(f32[72,128]{1,0:T(8,128)S(1)} %reduce_sum.39.mine_ref) | copy-start | bytes 110596
  112.3 10.5 %collective-permute-start.6 = (f32[72,128]{1,0:T(8,128)S(1)}, f32[72,128]{1,0:T(8,128)S(1)}, u32[]{:S(2)}, u32[]{:S(2)}) collective-permute-start(f32[72,128]{1,0:T(8,128)S(1)} %reduce_sum.39.mine_ref), channel_id=1, source_target_pairs={{4,256},{5,257},{6,258},{7,259},{12,264},{13,265},{14,266},{15,267... | collective-permute-start | bytes 110600 | tf_op jit(solution)/shard_map/ppermute | solution.py:31
  122.8 0.6 copy-start.4
